TPU v7x, 32 devices: a whole 2x2x4 slice. The times are simulated.
32 devices in a mesh: seq: 8 (over z, x), user: 4 (over y, core).
Axes of the slice: x: 2, y: 2, z: 4, core: 2. Of those that a mesh axis runs over, the one named last changes fastest.
Arguments:
- query: bfloat16 [4, 4096, 512], P('user', 'seq'), may hold values from -6 to 6
- key: bfloat16 [4, 4096, 512], P('user', 'seq'), may hold values from -6 to 6
- value: bfloat16 [4, 4096, 512], P('user', 'seq'), may hold values from -6 to 6
- gate: bfloat16 [4, 4096, 512], P('user', 'seq'), may hold values from -6 to 6
- history: bfloat16 [4, 4096, 128], P('user', 'seq'), may hold values from -6 to 6
- w_out: bfloat16 [512, 128], replicated, may hold values from -0.25 to 0.25
- table: bfloat16 [131072, 128], P(('seq', 'user')), may hold values from -0.5 to 0.5
- item_owner: int32 [4, 4096, 5], P('user', 'seq'), may hold values from 0 to 31, all different within a row; in each aligned block of 512 rows (0 to 511, 512 to 1023, ..., all dimensions but the last counted through in order) at most 120 rows name the same one
- item_row: int32 [4, 4096, 5], P('user', 'seq'), may hold values from 0 to 4095
- global_blocks: int32 [4, 2], P('user'), may hold values from 0 to 31, as said below
- lengths: int32 [4], replicated, may hold values from 1024 to 4096, as said below
Outputs:
- d_query: bfloat16 [4, 4096, 512], P('user', 'seq')
- d_key: bfloat16 [4, 4096, 512], P('user', 'seq')
- d_value: bfloat16 [4, 4096, 512], P('user', 'seq')
- d_gate: bfloat16 [4, 4096, 512], P('user', 'seq')
- table_grad: float32 [131072, 128], P(('seq', 'user'))
Inputs may be any that keep to these rules, and one draw needn't show every extreme that they name: `item_owner`: in the events of one device (512 aligned events of one user), no owner is named by more than 120 entries, a bound that some block reaches; the 5 owners of one event differ. `global_blocks`: the 2 block numbers of one user differ; the first lies among the blocks of the first 512 events. `lengths`: some user's length is 4096.
All inputs are finite; a program needn't handle non-finite values.
Results may differ from a plain program's by a relative error of at most 0.023.
Values may be sent and summed in bfloat16 or wider, within the bound.
A program may use at most 128 MiB of HBM per device.

v0:
```python
import math

import jax
import jax.numpy as jnp
from jax import lax
from jax.sharding import PartitionSpec as P

HEADS = 8
HEAD_DIM = 64
BLK = 128
GLOB = 2


def from_behind(block, axis, distance):
    devices = range(lax.axis_size(axis))
    route = [(i - distance, i) for i in devices if i - distance in devices]
    return lax.ppermute(block, axis, route)


def product(form, left, right):
    return jnp.einsum(form, left, right, preferred_element_type=jnp.float32)


def key_mask(block, gids, length):
    offs = jnp.arange(BLK, dtype=jnp.int32)
    q_pos = block * BLK + offs
    prev_pos = (block - 1) * BLK + offs
    own_pos = block * BLK + offs
    glob_pos = gids[:, None] * BLK + offs[None, :]
    prev_ok = (prev_pos >= 0) & (prev_pos < length)
    own_ok = (own_pos[None, :] <= q_pos[:, None]) & (own_pos[None, :] < length)
    glob_ok = ((gids[:, None] < block - 1) & (glob_pos < length)).reshape(-1)
    mask = jnp.concatenate(
        [
            jnp.broadcast_to(prev_ok[None, :], (BLK, BLK)),
            own_ok,
            jnp.broadcast_to(glob_ok[None, :], (BLK, GLOB * BLK)),
        ],
        axis=1,
    )
    return mask.astype(jnp.float32)


def split_heads(rows):
    return rows.reshape(rows.shape[0], HEADS, HEAD_DIM)


def attend_forward(q_blk, keys, mask):
    width = q_blk.shape[1]
    heads = split_heads(q_blk)
    kk = split_heads(keys[:, :width])
    vv = split_heads(keys[:, width:])
    scores = product("qhd,khd->hqk", heads, kk) * HEAD_DIM ** (-0.5)
    probs = (jax.nn.silu(scores) * mask[None]).astype(jnp.bfloat16)
    return product("hqk,khd->qhd", probs, vv).reshape(q_blk.shape[0], width)


def attend_backward(q_blk, keys, mask, grad_out):
    width = q_blk.shape[1]
    scale = HEAD_DIM ** (-0.5)
    heads = split_heads(q_blk)
    kk = split_heads(keys[:, :width])
    vv = split_heads(keys[:, width:])
    grads = split_heads(grad_out)
    scores = product("qhd,khd->hqk", heads, kk) * scale
    probs = (jax.nn.silu(scores) * mask[None]).astype(jnp.bfloat16)
    d_probs = product("qhd,khd->hqk", grads, vv)
    d_val = product("hqk,qhd->khd", probs, grads)
    sig = jax.nn.sigmoid(scores)
    d_scores = (d_probs * sig * (1.0 + scores * (1.0 - sig)) * mask[None] * scale).astype(
        jnp.bfloat16
    )
    d_q = product("hqk,khd->qhd", d_scores, kk)
    d_k = product("hqk,qhd->khd", d_scores, heads)
    count = keys.shape[0]
    return (
        d_q.reshape(q_blk.shape[0], width),
        jnp.concatenate([d_k.reshape(count, width), d_val.reshape(count, width)], axis=1),
    )


def middle(attn, gate, history, w_out, emb, valid):
    mean = jnp.mean(attn, axis=1, keepdims=True)
    centered = attn - mean
    var = jnp.mean(centered * centered, axis=1, keepdims=True)
    inv = lax.rsqrt(var + 1e-05)
    normed = centered * inv
    gate_f = gate.astype(jnp.float32)
    gated = (normed * gate_f).astype(jnp.bfloat16)
    user_vec = jnp.dot(gated, w_out, preferred_element_type=jnp.float32) + history.astype(
        jnp.float32
    )
    emb_f = emb.astype(jnp.float32)
    score = jnp.einsum("re,rje->rj", user_vec, emb_f)
    side = jax.nn.sigmoid(score[:, 1:] - score[:, :1]) * valid[:, None]
    coef = jnp.concatenate([-jnp.sum(side, axis=1, keepdims=True), side], axis=1)
    d_user = jnp.einsum("rj,rje->re", coef, emb_f).astype(jnp.bfloat16)
    d_emb = coef[:, :, None] * user_vec[:, None, :]
    d_gated = lax.dot_general(
        d_user, w_out, (((1,), (1,)), ((), ())), preferred_element_type=jnp.float32
    )
    d_gate = (d_gated * normed).astype(jnp.bfloat16)
    dn = d_gated * gate_f
    d_attn = (
        dn
        - jnp.mean(dn, axis=1, keepdims=True)
        - normed * jnp.mean(dn * normed, axis=1, keepdims=True)
    ) * inv
    return (d_attn.astype(jnp.bfloat16), d_gate, d_emb)


def on_device(
    query, key, value, gate, history, w_out, table, item_owner, item_row, global_blocks, lengths
):
    q_all = query[0]
    events = q_all.shape[0]
    width = q_all.shape[1]
    nbd = events // BLK
    seq_idx = lax.axis_index("seq")
    user_idx = lax.axis_index("user")
    length = lax.dynamic_slice_in_dim(lengths, user_idx, 1)[0]
    gids = global_blocks[0]
    base = seq_idx * nbd
    kv = jnp.concatenate([key[0], value[0]], axis=1)
    previous = from_behind(kv[events - BLK :], "seq", 1)
    holder = gids // nbd
    local_block = gids % nbd
    held = (holder == seq_idx).astype(jnp.float32)
    pieces = jnp.stack(
        [lax.dynamic_slice_in_dim(kv, local_block[index] * BLK, BLK, 0) for index in range(GLOB)]
    ).astype(jnp.float32)
    glob = lax.psum((pieces * held[:, None, None]).astype(jnp.bfloat16), "seq")
    kv_blocks = jnp.concatenate([previous[None], kv.reshape(nbd, BLK, 2 * width)], axis=0)
    keys_all = jnp.concatenate(
        [
            kv_blocks[:nbd, None],
            kv_blocks[1:, None],
            jnp.broadcast_to(glob[None], (nbd, GLOB, BLK, 2 * width)),
        ],
        axis=1,
    ).reshape(nbd, (2 + GLOB) * BLK, 2 * width)
    block_ids = base + jnp.arange(nbd, dtype=jnp.int32)
    masks = jax.vmap(key_mask, (0, None, None))(block_ids, gids, length)
    group = math.gcd(nbd, max(1, 512 // BLK))
    ngroups = nbd // group
    q_groups = q_all.reshape(ngroups, group, BLK, width)
    key_groups = keys_all.reshape(ngroups, group, (2 + GLOB) * BLK, 2 * width)
    mask_groups = masks.reshape(ngroups, group, BLK, (2 + GLOB) * BLK)
    firsts = block_ids.reshape(ngroups, group)[:, 0]

    def forward_group(inputs):
        q_grp, key_grp, mask_grp, first = inputs
        return jax.vmap(attend_forward)(q_grp, key_grp, mask_grp)

    attn = lax.map(forward_group, (q_groups, key_groups, mask_groups, firsts)).reshape(
        events, width
    )
    ndev = lax.axis_size(("seq", "user"))
    cap = max(2, 15 * events // (2 * ndev))
    dest = item_owner[0].reshape(-1)
    rows_wanted = item_row[0].reshape(-1)
    onehot = (dest[:, None] == jnp.arange(ndev, dtype=jnp.int32)[None, :]).astype(jnp.int32)
    slot = jnp.sum((jnp.cumsum(onehot, axis=0) - onehot) * onehot, axis=1)
    requests = jnp.full((ndev, cap), -1, jnp.int32).at[dest, slot].set(rows_wanted)
    asked = lax.all_to_all(requests, ("seq", "user"), split_axis=0, concat_axis=0, tiled=True)
    found = jnp.where(
        (asked >= 0)[..., None], table[jnp.maximum(asked, 0)], jnp.zeros((), jnp.bfloat16)
    )
    returned = lax.all_to_all(found, ("seq", "user"), split_axis=0, concat_axis=0, tiled=True)
    emb = returned[dest, slot].reshape(events, -1, returned.shape[2])
    valid = (base * BLK + jnp.arange(events, dtype=jnp.int32) < length).astype(jnp.float32)
    d_attn, d_gate, d_emb = middle(attn, gate[0], history[0], w_out, emb, valid)
    grad_groups = d_attn.reshape(ngroups, group, BLK, width)

    def backward_group(inputs):
        q_grp, key_grp, mask_grp, grad_grp, first = inputs
        return jax.vmap(attend_backward)(q_grp, key_grp, mask_grp, grad_grp)

    d_q, d_keys = lax.map(backward_group, (q_groups, key_groups, mask_groups, grad_groups, firsts))
    d_keys = d_keys.reshape(nbd, 2 + GLOB, BLK, 2 * width)
    d_blocks = jnp.zeros((nbd + 1, BLK, 2 * width), jnp.float32)
    d_blocks = d_blocks.at[:nbd].add(d_keys[:, 0]).at[1:].add(d_keys[:, 1])
    d_glob = jnp.sum(d_keys[:, 2:], axis=0)
    edge = from_behind(d_blocks[0].astype(jnp.bfloat16), "seq", -1).astype(jnp.float32)
    glob_total = lax.psum(d_glob.astype(jnp.bfloat16), "seq").astype(jnp.float32)
    local = d_blocks[1:].reshape(events, 2 * width)
    local = local.at[events - BLK :].add(edge)
    for index in range(GLOB):
        place = local_block[index] * BLK
        current = lax.dynamic_slice_in_dim(local, place, BLK, 0)
        local = lax.dynamic_update_slice_in_dim(
            local, current + glob_total[index] * held[index], place, 0
        )
    outgoing = (
        jnp.zeros((ndev, cap, d_emb.shape[2]), jnp.float32)
        .at[dest, slot]
        .set(d_emb.reshape(-1, d_emb.shape[2]))
    )
    incoming = lax.all_to_all(
        outgoing.astype(jnp.bfloat16), ("seq", "user"), split_axis=0, concat_axis=0, tiled=True
    ).astype(outgoing.dtype)
    table_grad = (
        jnp.zeros((table.shape[0], table.shape[1]), jnp.float32)
        .at[jnp.maximum(asked, 0).reshape(-1)]
        .add(incoming.reshape(-1, incoming.shape[2]))
    )
    d_query = d_q.reshape(events, width).astype(jnp.bfloat16)
    d_key = local[:, :width].astype(jnp.bfloat16)
    d_value = local[:, width:].astype(jnp.bfloat16)
    return (d_query[None], d_key[None], d_value[None], d_gate[None], table_grad)


def solution(mesh):
    return jax.shard_map(
        on_device,
        mesh=mesh,
        in_specs=(
            P("user", "seq", None),
            P("user", "seq", None),
            P("user", "seq", None),
            P("user", "seq", None),
            P("user", "seq", None),
            P(),
            P(("seq", "user"), None),
            P("user", "seq", None),
            P("user", "seq", None),
            P("user", None),
            P(),
        ),
        out_specs=(
            P("user", "seq", None),
            P("user", "seq", None),
            P("user", "seq", None),
            P("user", "seq", None),
            P(("seq", "user"), None),
        ),
        check_vma=False,
    )
```

profile of v0, /device:TPU:0, one launch (start us, length us, event | category | flops | bytes accessed | tf_op | source)
XLA Modules:
  0.0 320.5 jit_solution(9615246844623259000)
XLA Ops:
  10.5 1.3 fusion.50
  12.8 5.5 %collective-permute-start = (bf16[128,1024]{1,0:T(8,128)(2,1)S(1)}, bf16[128,1024]{1,0:T(8,128)(2,1)}, u32[]{:S(2)}, u32[]{:S(2)}) collective-permute-start(bf16[128,1024]{1,0:T(8,128)(2,1)S(1)} %get-tuple-element.109), channel_id=1, source_target_pairs={{0,4},{4,8},{8,12},{12,16},{16,20},{20,24},{24,28},{1,5},{5,9},{9,... | collective-permute-start | bytes 786440 | tf_op jit(solution)/shard_map/ppermute | solution.py:17
  19.3 9.2 %reduce-window.6 = s32[32,20,128]{2,1,0:T(8,128)S(1)} reduce-window(s32[32,20,128]{2,1,0:T(8,128)S(1)} %fusion.44, s32[]{:T(128)} %constant.179.clone.1), window={size=1x1x128 pad=0_0x0_0x127_0}, to_apply=%region_3.4 | reduce-window | flops 10403840 | bytes 655364 | tf_op jit(solution)/shard_map/reduce-window
  30.1 9.9 %scatter_custom_fusion.1 = s32[3840]{0:T(1024)S(1)} fusion(s32[2560]{0:T(1024)S(1)} %broadcast_select_fusion.1, s32[2560]{0:T(1024)S(1)} %reshape.599, s32[]{:T(128)} %constant.186.clone.1), kind=kCustom, calls=%fused_computation.120 | custom fusion | bytes 15364
  40.7 4.2 %all-to-all-start = ((s32[32,1,120]{2,1,0:T(1,128)}), s32[32,1,120]{2,1,0:T(1,128)S(1)}, u32[]{:S(2)}, u32[]{:S(2)}) async-start(s32[32,1,120]{2,1,0:T(1,128)} %all_to_all.12), calls=%async_computation | async-start | bytes 32768 | tf_op jit(solution)/shard_map/all_to_all | solution.py:165
  47.8 1.1 pad_maximum_fusion.4
  51.3 3.7 %copy.91 = bf16[4,1,128,1024]{2,1,3,0:T(2,128)(2,1)} copy(bf16[4,1,128,1024]{3,2,0,1:T(8,128)(2,1)S(1)} %copy-done.15) | data formatting | bytes 2097152 | tf_op jit(solution)/shard_map/concatenate | solution.py:124
  55.0 1.6 reshape.617
  56.7 1.4 copy.93
  58.1 1.3 copy.96
  59.5 7.5 %gather_fusion = bf16[3840,128]{1,0:T(8,128)(2,1)S(1)} fusion(bf16[4096,128]{1,0:T(8,128)(2,1)S(1)} %copy-done, s32[4096]{0:T(1024)S(1)} %pad_clamp_fusion), kind=kCustom, calls=%fused_computation | custom fusion | bytes 1981440 | tf_op jit(solution)/shard_map/gather | solution.py:167
  67.0 2.1 broadcast_select_fusion
  69.0 6.0 %all-to-all-start.1 = ((bf16[32,120,128]{2,1,0:T(8,128)(2,1)}), bf16[32,120,128]{2,1,0:T(8,128)(2,1)S(1)}, u32[]{:S(2)}, u32[]{:S(2)}) async-start(bf16[32,120,128]{2,1,0:T(8,128)(2,1)} %broadcast_select_fusion), calls=%async_computation.1 | async-start | bytes 1966080 | tf_op jit(solution)/shard_map/all_to_all | solution.py:169
  75.1 2.1 fusion.23
  77.1 6.0 %copy.90 = bf16[4,1,128,1024]{2,1,3,0:T(2,128)(2,1)} copy(bf16[4,1,128,1024]{3,2,0,1:T(8,128)(2,1)} %fusion.23) | data formatting | bytes 2097152 | tf_op jit(solution)/shard_map/broadcast_in_dim | solution.py:136
  83.1 10.0 %all-reduce.4.cloned.1.call-done = bf16[2,128,1024]{2,1,0:T(8,128)(2,1)} async-done(((bf16[2,128,1024]{2,1,0:T(8,128)(2,1)}), bf16[2,128,1024]{2,1,0:T(8,128)(2,1)}) %all-reduce.4.cloned.1.call-update) | async-done | bytes 524304 | tf_op jit(solution)/shard_map/psum | solution.py:132
  93.1 1.3 copy.89
  94.4 1.1 broadcast_in_dim.42
  96.0 9.1 %pad_maximum_fusion.1 = bf16[4,4,128,1024]{2,1,3,0:T(4,128)(2,1)} fusion(bf16[4,2,128,1024]{2,1,3,0:T(2,128)(2,1)S(1)} %broadcast_in_dim.42, bf16[4,1,128,1024]{2,1,3,0:T(2,128)(2,1)} %copy.91, bf16[4,1,128,1024]{2,1,3,0:T(2,128)(2,1)S(1)} %copy-done.8), kind=kLoop, calls=%fused_computation.26 | loop fusion | flops 12582912 | bytes 8388608 | tf_op jit(solution)/shard_map/concatenate | solution.py:134
  105.1 7.2 %squeeze.51 = bf16[4,512,1024]{1,2,0:T(8,128)(2,1)} reshape(bf16[4,4,128,1024]{2,1,3,0:T(4,128)(2,1)} %pad_maximum_fusion.1) | data formatting | bytes 8388608 | tf_op jit(solution)/shard_map/while/body/jit(dynamic_index_in_dim)/squeeze | solution.py:155
  112.3 2.8 fusion.74
  115.2 5.4 %fusion.4 = (bf16[4,8,128,512]{2,3,1,0:T(8,128)(2,1)S(1)}, f32[4,8,512,128]{3,2,1,0:T(8,128)}) fusion(f32[4,128,512]{1,2,0:T(8,128)S(1)} %copy-done.19, bf16[4,512,8,64]{1,3,2,0:T(8,128)(2,1)S(1)} %bitcast.217, bf16[4,128,8,64]{1,3,2,0:T(8,128)(2,1)S(1)} %copy-done.16), kind=kOutput, calls=%fused_computation.18 | convolution fusion | flops 283115520 | bytes 16252928 | tf_op jit(solution)/shard_map/while/body/eval_jaxpr/vmap(qhd,khd->hqk)/dot_general | solution.py:21
  123.9 1.4 mul.237
  125.3 2.5 mul.238
  127.9 13.8 %gather_fusion.1 = bf16[2560,128]{1,0:T(8,128)(2,1)S(1)} fusion(bf16[32,120,128]{2,1,0:T(8,128)(2,1)S(1)} %all-to-all-done.1, s32[2560]{0:T(1024)S(1)} %get-tuple-element.101), kind=kCustom, calls=%fused_computation.1 | custom fusion | bytes 1331200 | tf_op jit(solution)/shard_map/gather | solution.py:170
  141.7 1.2 reshape.554
  142.9 1.9 fusion.78
  145.2 1.9 fusion.79
  147.6 1.2 fusion.28
  148.9 7.8 %fusion.9 = bf16[4,8,128,512]{2,3,1,0:T(8,128)(2,1)S(1)} fusion(f32[4,8,512,128]{3,2,1,0:T(8,128)} %get-tuple-element.122, f32[4,128,512]{1,2,0:T(8,128)} %add_convert_fusion, bf16[4,512,8,64]{1,3,2,0:T(8,128)(2,1)} %bitcast.220, bf16[4,128,8,64]{1,0,3,2:T(4,128)(2,1)S(1)} %reshape.555), kind=kOutput, calls=%fused_computation.23 | convolution fusion | flops 293601280 | bytes 16252928 | tf_op jit(solution)/shard_map/while/body/eval_jaxpr/vmap(qhd,khd->hqk)/dot_general | solution.py:21
  157.7 3.5 %convolution_bitcast_fusion.1 = f32[4,512,8,64]{1,3,2,0:T(8,128)} fusion(bf16[4,8,128,512]{2,3,1,0:T(8,128)(2,1)S(1)} %fusion.9, bf16[4,128,8,64]{1,3,2,0:T(8,128)(2,1)S(1)} %copy-done.17), kind=kOutput, calls=%fused_computation.29 | convolution fusion | flops 268435456 | bytes 8912896 | tf_op jit(solution)/shard_map/while/body/eval_jaxpr/vmap(hqk,qhd->khd)/dot_general | solution.py:21
  161.8 1.4 reshape.616
  163.2 5.3 %concatenate.61 = f32[4,4,128,512]{2,1,3,0:T(4,128)} reshape(f32[4,512,8,64]{1,3,2,0:T(8,128)} %convolution_bitcast_fusion.1) | data formatting | bytes 8388608 | tf_op jit(solution)/shard_map/while/body/eval_jaxpr/vmap()/concatenate | solution.py:78
  168.5 5.2 %copy.113 = f32[4,4,128,512]{3,2,1,0:T(8,128)} copy(f32[4,4,128,512]{2,1,3,0:T(4,128)} %concatenate.61) | data formatting | bytes 8388608 | tf_op jit(solution)/shard_map/while/body/eval_jaxpr/vmap()/concatenate | solution.py:78
  174.1 9.0 %scatter_custom_fusion.2 = f32[3840,128]{1,0:T(8,128)S(1)} fusion(s32[2560]{0:T(1024)} %copy-done.23, f32[2560,128]{1,0:T(8,128)} %mul.238, f32[]{:T(128)} %constant.193.clone.1, f32[2560]{0:T(1024)S(1)} %mul.235), kind=kCustom, calls=%fused_computation.46 | custom fusion | flops 327680 | bytes 3287552
  184.2 4.5 %all-to-all-start.2 = ((bf16[32,120,128]{2,1,0:T(8,128)(2,1)}), bf16[32,120,128]{2,1,0:T(8,128)(2,1)}, u32[]{:S(2)}, u32[]{:S(2)}) async-start(bf16[32,120,128]{2,1,0:T(8,128)(2,1)} %bitcast.55), calls=%async_computation.2 | async-start | bytes 1966080 | tf_op jit(solution)/shard_map/all_to_all | solution.py:199
  188.7 5.7 %convolution_bitcast_fusion = f32[4,512,8,64]{1,3,2,0:T(8,128)} fusion(bf16[4,8,128,512]{2,3,1,0:T(8,128)(2,1)} %copy-done.6, bf16[4,128,8,64]{1,0,3,2:T(4,128)(2,1)S(1)} %reshape.555), kind=kOutput, calls=%fused_computation.28 | convolution fusion | flops 268435456 | bytes 8912896 | tf_op jit(solution)/shard_map/while/body/eval_jaxpr/vmap(hqk,qhd->khd)/dot_general | solution.py:21
  194.4 5.3 %concatenate.62 = f32[4,4,128,512]{2,1,3,0:T(4,128)} reshape(f32[4,512,8,64]{1,3,2,0:T(8,128)} %convolution_bitcast_fusion) | data formatting | bytes 8388608 | tf_op jit(solution)/shard_map/while/body/eval_jaxpr/vmap()/concatenate | solution.py:78
  199.7 5.3 %copy.114 = f32[4,4,128,512]{3,2,1,0:T(8,128)} copy(f32[4,4,128,512]{2,1,3,0:T(4,128)} %concatenate.62) | data formatting | bytes 8388608 | tf_op jit(solution)/shard_map/while/body/eval_jaxpr/vmap()/concatenate | solution.py:78
  204.9 1.2 fusion.53
  206.2 1.8 collective-permute-start.1
  208.6 1.3 fusion.10
  209.9 1.9 fusion.13
  212.7 1.3 copy-done.5
  217.4 1.1 fusion.37
  218.5 65.7 %all-reduce.6.cloned.1.call-done = bf16[2,128,1024]{2,1,0:T(8,128)(2,1)} async-done(((bf16[2,128,1024]{2,1,0:T(8,128)(2,1)}), bf16[2,128,1024]{2,1,0:T(8,128)(2,1)}) %all-reduce.6.cloned.1.call-update) | async-done | bytes 524304 | tf_op jit(solution)/shard_map/psum | solution.py:185
  284.2 1.1 convert_element_type.122
  288.1 25.6 %scatter_custom_fusion = f32[4096,128]{1,0:T(8,128)} fusion(s32[3840]{0:T(1024)S(1)} %reshape.577, bf16[3840,128]{1,0:T(8,128)(2,1)} %bitcast.60, f32[]{:T(128)} %constant.193.clone.1), kind=kCustom, calls=%fused_computation.35 | custom fusion | flops 983040 | bytes 3080196 | tf_op jit(solution)/shard_map/scatter-add | solution.py:205
  (138 shorter events, 26.7 us)
Async XLA Ops:
  7.2 52.3 %copy-start = (bf16[4096,128]{1,0:T(8,128)(2,1)S(1)}, bf16[4096,128]{1,0:T(8,128)(2,1)}, u32[]{:S(2)}) copy-start(bf16[4096,128]{1,0:T(8,128)(2,1)} %param.23) | copy-start | bytes 3145732
  7.2 11.2 %copy-start.24 = (s32[1,512,5]{1,0,2:T(1,128)S(1)}, s32[1,512,5]{1,0,2:T(1,128)}, u32[]{:S(2)}) copy-start(s32[1,512,5]{1,0,2:T(1,128)} %param.24) | copy-start | bytes 30724
  7.2 85.9 %all-reduce.4.cloned.1.call-start = ((), (), s32[]{:S(2)}) async-start(), calls=%async_computation.3 | async-start | bytes 1048576 | tf_op jit(solution)/shard_map/psum | solution.py:132
  12.8 62.2 %collective-permute-start = (bf16[128,1024]{1,0:T(8,128)(2,1)S(1)}, bf16[128,1024]{1,0:T(8,128)(2,1)}, u32[]{:S(2)}, u32[]{:S(2)}) collective-permute-start(bf16[128,1024]{1,0:T(8,128)(2,1)S(1)} %get-tuple-element.109), channel_id=1, source_target_pairs={{0,4},{4,8},{8,12},{12,16},{16,20},{20,24},{24,28},{1,5},{5,9},{9,... | collective-permute-start | bytes 786440 | tf_op jit(solution)/shard_map/ppermute | solution.py:17
  18.7 10.7 %copy-start.27 = (s32[2]{0:T(128)S(1)}, s32[2]{0:T(128)}, u32[]{:S(2)}) copy-start(s32[2]{0:T(128)} %constant.213) | copy-start | bytes 28
  18.8 10.8 %copy-start.26 = (s32[2]{0:T(128)S(1)}, s32[2]{0:T(128)}, u32[]{:S(2)}) copy-start(s32[2]{0:T(128)} %constant.210) | copy-start | bytes 28
  18.8 10.9 %copy-start.25 = (s32[1,512,5]{1,0,2:T(1,128)S(1)}, s32[1,512,5]{1,0,2:T(1,128)}, u32[]{:S(2)}) copy-start(s32[1,512,5]{1,0,2:T(1,128)} %param.25) | copy-start | bytes 30724
  19.2 26.5 %copy-start.28 = (s32[4]{0:T(128)S(1)}, s32[4]{0:T(128)}, u32[]{:S(2)}) copy-start(s32[4]{0:T(128)} %param.27) | copy-start | bytes 52
  19.2 28.5 %copy-start.12 = (bf16[1,512,512]{2,1,0:T(8,128)(2,1)S(1)}, bf16[1,512,512]{2,1,0:T(8,128)(2,1)}, u32[]{:S(2)}) copy-start(bf16[1,512,512]{2,1,0:T(8,128)(2,1)} %param.18) | copy-start | bytes 1572868
  19.2 28.5 %copy-start.13 = (bf16[1,512,512]{2,1,0:T(8,128)(2,1)S(1)}, bf16[1,512,512]{2,1,0:T(8,128)(2,1)}, u32[]{:S(2)}) copy-start(bf16[1,512,512]{2,1,0:T(8,128)(2,1)} %param.19) | copy-start | bytes 1572868
  28.9 20.0 %copy-start.29 = (s32[1,2]{1,0:T(1,128)S(1)}, s32[1,2]{1,0:T(1,128)}, u32[]{:S(2)}) copy-start(s32[1,2]{1,0:T(1,128)} %param.26) | copy-start | bytes 28
  30.1 17.7 %copy-start.23 = (s32[2560]{0:T(1024)}, s32[2560]{0:T(1024)S(1)}, u32[]{:S(2)}) copy-start(s32[2560]{0:T(1024)S(1)} %broadcast_select_fusion.1) | copy-start | bytes 30724
  40.7 18.6 %all-to-all-start = ((s32[32,1,120]{2,1,0:T(1,128)}), s32[32,1,120]{2,1,0:T(1,128)S(1)}, u32[]{:S(2)}, u32[]{:S(2)}) async-start(s32[32,1,120]{2,1,0:T(1,128)} %all_to_all.12), calls=%async_computation | async-start | bytes 32768 | tf_op jit(solution)/shard_map/all_to_all | solution.py:165
  48.9 2.4 copy-start.15
  67.0 8.1 %copy-start.14 = (bf16[1,512,512]{2,1,0:T(8,128)(2,1)S(1)}, bf16[1,512,512]{2,1,0:T(8,128)(2,1)}, u32[]{:S(2)}) copy-start(bf16[1,512,512]{2,1,0:T(8,128)(2,1)} %param.19) | copy-start | bytes 1572868
  69.0 58.8 %all-to-all-start.1 = ((bf16[32,120,128]{2,1,0:T(8,128)(2,1)}), bf16[32,120,128]{2,1,0:T(8,128)(2,1)S(1)}, u32[]{:S(2)}, u32[]{:S(2)}) async-start(bf16[32,120,128]{2,1,0:T(8,128)(2,1)} %broadcast_select_fusion), calls=%async_computation.1 | async-start | bytes 1966080 | tf_op jit(solution)/shard_map/all_to_all | solution.py:169
  94.4 1.6 copy-start.8
  112.3 2.8 copy-start.16
  112.3 2.8 copy-start.19
  115.1 5.4 %copy-start.9 = (bf16[4,512,512]{1,2,0:T(8,128)(2,1)}, bf16[4,512,512]{1,2,0:T(8,128)(2,1)S(1)}, u32[]{:S(2)}) copy-start(bf16[4,512,512]{1,2,0:T(8,128)(2,1)S(1)} %get-tuple-element.104) | copy-start | bytes 6291460
  115.2 5.4 %copy-start.11 = (bf16[4,512,512]{1,2,0:T(8,128)(2,1)}, bf16[4,512,512]{1,2,0:T(8,128)(2,1)S(1)}, u32[]{:S(2)}) copy-start(bf16[4,512,512]{1,2,0:T(8,128)(2,1)S(1)} %get-tuple-element.103) | copy-start | bytes 6291460
  120.6 2.0 copy-start.6
  122.5 0.9 copy-start.20
  122.5 1.0 copy-start.22
  142.9 4.3 %copy-start.21 = (bf16[512,128]{1,0:T(8,128)(2,1)S(1)}, bf16[512,128]{1,0:T(8,128)(2,1)}, u32[]{:S(2)}) copy-start(bf16[512,128]{1,0:T(8,128)(2,1)} %param.22) | copy-start | bytes 393220
  148.9 7.8 %copy-start.10 = (bf16[4,512,512]{1,2,0:T(8,128)(2,1)S(1)}, bf16[4,512,512]{1,2,0:T(8,128)(2,1)}, u32[]{:S(2)}) copy-start(bf16[4,512,512]{1,2,0:T(8,128)(2,1)} %copy-done.9) | copy-start | bytes 6291460
  156.7 1.0 copy-start.17
  184.2 103.9 %all-to-all-start.2 = ((bf16[32,120,128]{2,1,0:T(8,128)(2,1)}), bf16[32,120,128]{2,1,0:T(8,128)(2,1)}, u32[]{:S(2)}, u32[]{:S(2)}) async-start(bf16[32,120,128]{2,1,0:T(8,128)(2,1)} %bitcast.55), calls=%async_computation.2 | async-start | bytes 1966080 | tf_op jit(solution)/shard_map/all_to_all | solution.py:199
  188.6 95.6 %all-reduce.6.cloned.1.call-start = ((), (), s32[]{:S(2)}) async-start(), calls=%async_computation.4 | async-start | bytes 1048576 | tf_op jit(solution)/shard_map/psum | solution.py:185
  204.9 3.0 copy-start.2
  204.9 3.6 %copy-start.4 = (f32[4,4,128,512]{3,2,1,0:T(8,128)S(1)}, f32[4,4,128,512]{3,2,1,0:T(8,128)}, u32[]{:S(2)}) copy-start(f32[4,4,128,512]{3,2,1,0:T(8,128)} %copy.114) | copy-start | bytes 12582916
  206.2 11.2 %collective-permute-start.1 = (bf16[128,1024]{1,0:T(8,128)(2,1)S(1)}, bf16[128,1024]{1,0:T(8,128)(2,1)S(1)}, u32[]{:S(2)}, u32[]{:S(2)}) collective-permute-start(bf16[128,1024]{1,0:T(8,128)(2,1)S(1)} %fusion.53), channel_id=1, source_target_pairs={{4,0},{8,4},{12,8},{16,12},{20,16},{24,20},{28,24},{5,1},{9,5},{13... | collective-permute-start | bytes 786440 | tf_op jit(solution)/shard_map/ppermute | solution.py:17
  209.9 2.8 copy-start.3
  209.9 4.1 %copy-start.5 = (f32[4,4,128,512]{3,2,1,0:T(8,128)S(1)}, f32[4,4,128,512]{3,2,1,0:T(8,128)}, u32[]{:S(2)}) copy-start(f32[4,4,128,512]{3,2,1,0:T(8,128)} %copy.114) | copy-start | bytes 12582916
  214.4 1.3 copy-start.7
  214.4 1.4 copy-start.18
  286.9 26.8 %copy-start.1 = (bf16[4096,128]{1,0:T(8,128)(2,1)S(1)}, bf16[4096,128]{1,0:T(8,128)(2,1)}, u32[]{:S(2)}) copy-start(bf16[4096,128]{1,0:T(8,128)(2,1)} %param.23) | copy-start | bytes 3145732
Sparse Core Ops, SparseCore 0:
  12.9 80.0 all-reduce.3
  210.0 74.1 all-reduce.5
where the time goes:
time: 322 us; the launch traced here: 320 us
  local copies, waits for them, and re-layouts  100 us (31%)
  other arithmetic  77.1 us (24%)
  waiting for transfers between devices  76.3 us (24%)
  matrix products  28.8 us (9%)
  starting transfers between devices  22.1 us (7%)
  between operations  16.1 us (5%)
    psum x1, waiting for transfers between devices, on_device(): lax.psum(d_glob.astype(jnp.bfloat16), 'seq').astype(jnp.float32)  65.7 us
    scatter-add x1, other arithmetic, on_device(): table_grad = jnp.zeros((table.shape[0], table.shape[1]), jnp.float32).at[...  25.6 us
    dot_general x6, matrix products, product(): return jnp.einsum(form, left, right, preferred_element_type=jnp.float32)  24.2 us
    concatenate x4, local copies, waits for them, and re-layouts, attend_backward(): jnp.concatenate([d_k.reshape(count, width), d_val.reshape(count, width)],...  21 us
    unnamed x68, local copies, waits for them, and re-layouts  20.6 us
    gather x1, local copies, waits for them, and re-layouts, on_device(): emb = returned[dest, slot].reshape(events, -1, returned.shape[2])  13.8 us
    psum x1, waiting for transfers between devices, on_device(): glob = lax.psum((pieces * held[:, None, None]).astype(jnp.bfloat16), 'seq')  9.97 us
    another operation x4, other arithmetic  9.68 us
  transfers between devices with their start and end apart: 7, of which 3 were waited for; matrix products, arithmetic and copies ran while one was open for 35% of the time, Pallas kernels for 0%

commit v1 on v0

v1 whole, which is shorter than its diff:
```python
import functools

import jax
import jax.numpy as jnp
from jax import lax
from jax.experimental import pallas as pl
from jax.experimental.pallas import tpu as pltpu
from jax.sharding import PartitionSpec as P

HEADS = 8
HEAD_DIM = 64
BLK = 128
GLOB = 2
PAIR = 2 * HEAD_DIM
HI = 512
F32 = jnp.float32
BF16 = jnp.bfloat16
VMEM = pl.BlockSpec(memory_space=pltpu.VMEM)
SMEM = pl.BlockSpec(memory_space=pltpu.SMEM)
NT = (((1,), (1,)), ((), ()))
TN = (((0,), (0,)), ((), ()))
LIMIT = 50 * 1024 * 1024


def iota(shape, axis):
    return lax.broadcasted_iota(jnp.int32, shape, axis)


def mm(left, right):
    return jnp.dot(left, right, preferred_element_type=F32)


def dg(left, right, dims):
    return lax.dot_general(left, right, dims, preferred_element_type=F32)


def request_kernel(owner_ref, row_ref, slots_ref, req_ref):
    ndev, events = slots_ref.shape
    cap = req_ref.shape[1]
    dev = iota((ndev, events), 0)
    hits = [owner_ref[j : j + 1, :] == dev for j in range(owner_ref.shape[0])]
    named = functools.reduce(jnp.logical_or, hits)
    upper = (iota((events, events), 0) < iota((events, events), 1)).astype(BF16)
    rank = mm(named.astype(BF16), upper)
    slots_ref[...] = jnp.where(named, rank, -1.0)
    high = jnp.zeros((ndev, cap), F32)
    low = jnp.zeros((ndev, cap), F32)
    place = iota((cap, events), 0)
    for j, hit in enumerate(hits):
        slot = jnp.sum(jnp.where(hit, rank, 0.0), axis=0, keepdims=True).astype(jnp.int32)
        chosen = (place == slot).astype(BF16)
        code = row_ref[j : j + 1, :] + 1
        high += dg(jnp.where(hit, (code // 64).astype(F32), 0.0).astype(BF16), chosen, NT)
        low += dg(jnp.where(hit, (code % 64).astype(F32), 0.0).astype(BF16), chosen, NT)
    req_ref[...] = (high * 64.0 + low).astype(jnp.int32) - 1


def gather_kernel(asked_ref, table_ref, out_ref):
    cap, ndev = asked_ref.shape
    width = table_ref.shape[1]
    parts = table_ref.shape[0] // HI
    for d in range(ndev):
        ask = asked_ref[:, d : d + 1]
        part = ask // HI
        chosen = (jnp.broadcast_to(ask - part * HI, (cap, HI)) == iota((cap, HI), 1)).astype(BF16)
        part_b = jnp.broadcast_to(part, (cap, width))
        empty = jnp.broadcast_to(ask, (cap, width)) < 0
        rows = jnp.zeros((cap, width), F32)
        for k in range(parts):
            rows = jnp.where(part_b == k, mm(chosen, table_ref[k * HI : (k + 1) * HI, :]), rows)
        out_ref[d] = jnp.where(empty, 0.0, rows).astype(BF16)


def scatter_kernel(asked_ref, asked_row_ref, inc_ref, out_ref):
    ndev, cap, width = inc_ref.shape
    parts = out_ref.shape[0] // HI
    group = max(1, 512 // cap)
    for first in range(0, ndev, group):
        row = asked_row_ref[:, first * cap : (first + group) * cap]
        chosen = (row % HI == iota((HI, group * cap), 0)).astype(BF16)
        pieces = []
        for d in range(first, first + group):
            part_b = jnp.broadcast_to(asked_ref[:, d : d + 1], (cap, width)) // HI
            inc = inc_ref[d].astype(F32)
            wide = [jnp.where(part_b == k, inc, 0.0).astype(BF16) for k in range(parts)]
            pieces.append(jnp.concatenate(wide, axis=1))
        total = mm(chosen, jnp.concatenate(pieces, axis=0))
        for k in range(parts):
            rows = slice(k * HI, (k + 1) * HI)
            piece = total[:, k * width : (k + 1) * width]
            if first == 0:
                out_ref[rows, :] = piece
            else:
                out_ref[rows, :] += piece


def stack_pair(rows):
    lane = iota(rows.shape, 1)
    zero = jnp.zeros_like(rows)
    return jnp.concatenate(
        [jnp.where(lane < HEAD_DIM, rows, zero), jnp.where(lane < HEAD_DIM, zero, rows)], axis=0
    )


def merge_pair(stacked):
    half = stacked.shape[0] // 2
    lane = iota((half, stacked.shape[1]), 1)
    return jnp.where(lane < HEAD_DIM, stacked[:half], stacked[half:])


def visible(info_ref, b):
    block, length = info_ref[0] + b, info_ref[1]
    query = iota((2 * BLK, BLK), 0) % BLK
    key = iota((2 * BLK, BLK), 1)
    prev = (key + (block - 1) * BLK < length) & (block > 0)
    own = (key <= query) & (key + block * BLK < length)
    globs = [
        (key + info_ref[2 + g] * BLK < length) & (info_ref[2 + g] < block - 1) for g in range(GLOB)
    ]
    return jnp.concatenate([m.astype(F32) for m in [prev, own] + globs], axis=1)


def forward_kernel(info_ref, q_ref, k_ref, v_ref, prev_ref, glob_ref, attn_ref):
    events, width = q_ref.shape
    for b in range(events // BLK):
        rows = slice(b * BLK, (b + 1) * BLK)
        mask = visible(info_ref, b)
        for p in range(width // PAIR):
            cols = slice(p * PAIR, (p + 1) * PAIR)
            vcols = slice(width + p * PAIR, width + (p + 1) * PAIR)
            kk = jnp.concatenate(
                [
                    prev_ref[:, cols] if b == 0 else k_ref[(b - 1) * BLK : b * BLK, cols],
                    k_ref[rows, cols],
                ]
                + [glob_ref[g, :, cols] for g in range(GLOB)],
                axis=0,
            )
            vv = jnp.concatenate(
                [
                    prev_ref[:, vcols] if b == 0 else v_ref[(b - 1) * BLK : b * BLK, cols],
                    v_ref[rows, cols],
                ]
                + [glob_ref[g, :, vcols] for g in range(GLOB)],
                axis=0,
            )
            qs = stack_pair(q_ref[rows, cols]) * HEAD_DIM**-0.5
            scores = dg(qs, kk, NT)
            sig = 0.5 * jnp.tanh(0.5 * scores) + 0.5
            probs = (scores * sig * mask).astype(BF16)
            attn_ref[rows, cols] = merge_pair(mm(probs, vv))


def middle_kernel(
    info_ref, attn_ref, gate_ref, hist_ref, w_ref, ret_ref, slots_ref, owner_ref,
    d_attn_ref, d_gate_ref, out_ref,
):
    ndev, cap, emb = ret_ref.shape
    events = attn_ref.shape[0]
    attn = attn_ref[...]
    centered = attn - jnp.mean(attn, axis=1, keepdims=True)
    inv = lax.rsqrt(jnp.mean(centered * centered, axis=1, keepdims=True) + 1e-05)
    normed = centered * inv
    gate = gate_ref[...].astype(F32)
    user = mm((normed * gate).astype(BF16), w_ref[...]) + hist_ref[...].astype(F32)
    user_hi = user.astype(BF16)
    user_lo = (user - user_hi.astype(F32)).astype(BF16)
    slots = slots_ref[...].astype(jnp.int32)
    place = iota((cap, events), 0)
    score = []
    for d in range(ndev):
        rows = ret_ref[d]
        full = dg(rows, user_hi, NT) + dg(rows, user_lo, NT)
        score.append(
            jnp.sum(jnp.where(place == slots[d : d + 1], full, 0.0), axis=0, keepdims=True)
        )
    score = jnp.concatenate(score, axis=0)
    positive = owner_ref[0:1, :] == iota((ndev, events), 0)
    first = jnp.sum(jnp.where(positive, score, 0.0), axis=0, keepdims=True)
    valid = info_ref[0] * BLK + iota((ndev, events), 1) < info_ref[1]
    side = jnp.where((slots >= 0) & valid & ~positive, jax.nn.sigmoid(score - first), 0.0)
    coef = jnp.where(positive, -jnp.sum(side, axis=0, keepdims=True), side)
    d_user = jnp.zeros((emb, events), F32)
    for d in range(ndev):
        weights = jnp.where(place == slots[d : d + 1], coef[d : d + 1], 0.0).astype(BF16)
        out_ref[d] = mm(weights, user_hi).astype(BF16)
        d_user += dg(ret_ref[d], weights, TN)
    d_gated = dg(d_user.T.astype(BF16), w_ref[...], NT)
    d_gate_ref[...] = (d_gated * normed).astype(BF16)
    dn = d_gated * gate
    d_attn_ref[...] = (
        (
            dn
            - jnp.mean(dn, axis=1, keepdims=True)
            - normed * jnp.mean(dn * normed, axis=1, keepdims=True)
        )
        * inv
    ).astype(BF16)


def backward_kernel(
    info_ref, q_ref, k_ref, v_ref, prev_ref, glob_ref, g_ref,
    dq_ref, dkv_ref, d_prev_ref, d_glob_ref, acc_ref,
):
    events, width = q_ref.shape
    nbd = events // BLK
    for b in range(nbd):
        rows = slice(b * BLK, (b + 1) * BLK)
        before = slice((b - 1) * BLK, b * BLK)
        mask = visible(info_ref, b)
        for p in range(width // PAIR):
            cols = slice(p * PAIR, (p + 1) * PAIR)
            vcols = slice(width + p * PAIR, width + (p + 1) * PAIR)
            kk = jnp.concatenate(
                [prev_ref[:, cols] if b == 0 else k_ref[before, cols], k_ref[rows, cols]]
                + [glob_ref[g, :, cols] for g in range(GLOB)],
                axis=0,
            )
            vv = jnp.concatenate(
                [prev_ref[:, vcols] if b == 0 else v_ref[before, cols], v_ref[rows, cols]]
                + [glob_ref[g, :, vcols] for g in range(GLOB)],
                axis=0,
            )
            qs = stack_pair(q_ref[rows, cols]) * HEAD_DIM**-0.5
            gs = stack_pair(g_ref[rows, cols])
            scores = dg(qs, kk, NT)
            sig = 0.5 * jnp.tanh(0.5 * scores) + 0.5
            masked = sig * mask
            probs = (scores * masked).astype(BF16)
            slope = masked * (1.0 + scores * (1.0 - sig))
            d_scores = (dg(gs, vv, NT) * slope).astype(BF16)
            dq_ref[rows, cols] = (merge_pair(mm(d_scores, kk)) * HEAD_DIM**-0.5).astype(BF16)
            for grad, at in ((dg(d_scores, qs, TN), cols), (dg(probs, gs, TN), vcols)):
                if b == 0:
                    d_prev_ref[:, at] = grad[:BLK].astype(BF16)
                else:
                    dkv_ref[before, at] += grad[:BLK]
                dkv_ref[rows, at] = grad[BLK : 2 * BLK]
                for g in range(GLOB):
                    piece = grad[(2 + g) * BLK : (3 + g) * BLK]
                    if b == 0:
                        acc_ref[g, :, at] = piece
                    else:
                        acc_ref[g, :, at] += piece
    d_glob_ref[...] = acc_ref[...].astype(BF16)


def call(kernel, outs, in_specs, scratch=(), flops=1 << 30):
    return pl.pallas_call(
        kernel,
        out_shape=[jax.ShapeDtypeStruct(shape, dtype) for shape, dtype in outs],
        in_specs=in_specs,
        out_specs=[VMEM] * len(outs),
        scratch_shapes=list(scratch),
        compiler_params=pltpu.CompilerParams(vmem_limit_bytes=LIMIT),
        cost_estimate=pl.CostEstimate(flops=flops, bytes_accessed=1 << 22, transcendentals=0),
    )


def from_behind(block, axis, distance):
    devices = range(lax.axis_size(axis))
    route = [(i - distance, i) for i in devices if i - distance in devices]
    return lax.ppermute(block, axis, route)


def on_device(
    query, key, value, gate, history, w_out, table, item_owner, item_row, global_blocks, lengths
):
    q, k, v = query[0], key[0], value[0]
    events, width = q.shape
    nbd = events // BLK
    emb = table.shape[1]
    axes = ("seq", "user")
    ndev = lax.axis_size(axes)
    cap = -(-max(2, 15 * events // (2 * ndev)) // 16) * 16
    seq_idx = lax.axis_index("seq")
    length = lax.dynamic_slice_in_dim(lengths, lax.axis_index("user"), 1)[0]
    gids = global_blocks[0]
    base = seq_idx * nbd
    info = jnp.concatenate([jnp.stack([base, length]), gids]).astype(jnp.int32)
    owner_t, row_t = item_owner[0].T, item_row[0].T

    slots, requests = call(
        request_kernel, [((ndev, events), F32), ((ndev, cap), jnp.int32)], [VMEM] * 2
    )(owner_t, row_t)
    asked = lax.all_to_all(requests, axes, split_axis=0, concat_axis=0, tiled=True)

    previous = from_behind(jnp.concatenate([k[events - BLK :], v[events - BLK :]], axis=1), "seq", 1)
    holder, local_block = gids // nbd, gids % nbd
    held = holder == seq_idx
    pieces = jnp.stack(
        [
            jnp.concatenate(
                [lax.dynamic_slice_in_dim(x, local_block[g] * BLK, BLK, 0) for x in (k, v)], axis=1
            )
            for g in range(GLOB)
        ]
    )
    glob = lax.psum(jnp.where(held[:, None, None], pieces, jnp.zeros((), BF16)), "seq")

    asked_t = asked.T
    (found,) = call(gather_kernel, [((ndev, cap, emb), BF16)], [VMEM] * 2)(asked_t, table)
    returned = lax.all_to_all(found, axes, split_axis=0, concat_axis=0, tiled=True)

    (attn,) = call(forward_kernel, [((events, width), F32)], [SMEM] + [VMEM] * 5)(
        info, q, k, v, previous, glob
    )
    d_attn, d_gate, outgoing = call(
        middle_kernel,
        [((events, width), BF16), ((events, width), BF16), ((ndev, cap, emb), BF16)],
        [SMEM] + [VMEM] * 7,
    )(info, attn, gate[0], history[0], w_out, returned, slots, owner_t)
    incoming = lax.all_to_all(outgoing, axes, split_axis=0, concat_axis=0, tiled=True)

    d_q, local, d_prev, d_glob = call(
        backward_kernel,
        [
            ((events, width), BF16),
            ((events, 2 * width), F32),
            ((BLK, 2 * width), BF16),
            ((GLOB, BLK, 2 * width), BF16),
        ],
        [SMEM] + [VMEM] * 6,
        [pltpu.VMEM((GLOB, BLK, 2 * width), F32)],
    )(info, q, k, v, previous, glob, d_attn)
    edge = from_behind(d_prev, "seq", -1).astype(F32)
    glob_total = lax.psum(d_glob, "seq").astype(F32)
    blocks = local.reshape(nbd, BLK, 2 * width).at[nbd - 1].add(edge)
    here = (jnp.arange(nbd)[:, None] == local_block[None, :]) & held[None, :]
    for g in range(GLOB):
        blocks = blocks + jnp.where(here[:, g, None, None], glob_total[g][None], 0.0)
    local = blocks.reshape(events, 2 * width).astype(BF16)

    (table_grad,) = call(scatter_kernel, [(table.shape, F32)], [VMEM] * 3)(
        asked_t, asked.reshape(1, ndev * cap), incoming
    )
    return (d_q[None], local[None, :, :width], local[None, :, width:], d_gate[None], table_grad)


def solution(mesh):
    return jax.shard_map(
        on_device,
        mesh=mesh,
        in_specs=(
            P("user", "seq", None),
            P("user", "seq", None),
            P("user", "seq", None),
            P("user", "seq", None),
            P("user", "seq", None),
            P(),
            P(("seq", "user"), None),
            P("user", "seq", None),
            P("user", "seq", None),
            P("user", None),
            P(),
        ),
        out_specs=(
            P("user", "seq", None),
            P("user", "seq", None),
            P("user", "seq", None),
            P("user", "seq", None),
            P(("seq", "user"), None),
        ),
        check_vma=False,
    )
```

time: 322 us -> 251 us (0.78)
  local copies, waits for them, and re-layouts: 100 us -> 12.2 us
  waiting for transfers between devices: 76.3 us -> 147 us
  other arithmetic: 77.1 us -> 6.9 us
  Pallas kernels: 0 us -> 41 us
  matrix products: 28.8 us -> 0 us
  blocking collectives: 0 us -> 14.3 us
  starting transfers between devices: 22.1 us -> 12.9 us
    psum x2, waiting for transfers between devices: 75.7 us -> 129 us  [the longest x1 65.9 us: on_device(): lax.psum(jnp.where(held[:, None, None], pieces, jnp.zeros((), BF16)), 'seq')]
    pallas_call x0 -> x6, Pallas kernels: none -> 41 us  [the longest x1 10.6 us: on_device(): call(gather_kernel, [((ndev, cap, emb), BF16)], [VMEM] * 2)(asked_t, table)]
    dot_general x10 -> x0, matrix products: 28.8 us -> none  [the longest x6 24.2 us: product(): return jnp.einsum(form, left, right, preferred_element_type=jnp.float32)]
    concatenate x7 -> x0, local copies, waits for them, and re-layouts: 25.1 us -> none  [the longest x4 21 us: attend_backward(): jnp.concatenate([d_k.reshape(count, width), d_val.reshape(count, width)],...]
    scatter-add x2 -> x1, other arithmetic: 26.6 us -> 1.9 us  [on_device(): blocks = local.reshape(nbd, BLK, 2 * width).at[nbd - 1].add(edge)]
    gather x2 -> x0, local copies, waits for them, and re-layouts: 21.3 us -> none  [the longest x1 13.8 us: on_device(): emb = returned[dest, slot].reshape(events, -1, returned.shape[2])]
    ppermute x2, waiting for transfers between devices: 0.58 us -> 17.7 us  [from_behind(): return lax.ppermute(block, axis, route)]
    all_to_all x0 -> x1, blocking collectives: none -> 14.3 us  [on_device(): lax.all_to_all(requests, axes, split_axis=0, concat_axis=0, tiled=True)]
  transfers between devices with their start and end apart: 7 -> 6, of which waited for: 3 -> 4; matrix products, arithmetic and copies ran while one was open for 35% -> 5% of each run, Pallas kernels for 0% -> 6%
where the time goes in v1:
time: 251 us; the launch traced here: 250 us
  waiting for transfers between devices  147 us (59%)
  Pallas kernels  41 us (16%)
  between operations  15.6 us (6%)
  blocking collectives  14.3 us (6%)
  starting transfers between devices  12.9 us (5%)
  local copies, waits for them, and re-layouts  12.2 us (5%)
  other arithmetic  6.9 us (3%)
    psum x1, waiting for transfers between devices, on_device(): lax.psum(jnp.where(held[:, None, None], pieces, jnp.zeros((), BF16)), 'seq')  65.9 us
    psum x1, waiting for transfers between devices, on_device(): glob_total = lax.psum(d_glob, 'seq').astype(F32)  63.2 us
    ppermute x2, waiting for transfers between devices, from_behind(): return lax.ppermute(block, axis, route)  17.7 us
    all_to_all x1, blocking collectives, on_device(): lax.all_to_all(requests, axes, split_axis=0, concat_axis=0, tiled=True)  14.3 us
    pallas_call x1, Pallas kernels, on_device(): call(gather_kernel, [((ndev, cap, emb), BF16)], [VMEM] * 2)(asked_t, table)  10.6 us
    pallas_call x1, Pallas kernels, on_device(): call(backward_kernel, [((events, width), BF16), ((events, 2 * width), F32...  10.3 us
    unnamed x33, local copies, waits for them, and re-layouts  9.79 us
    pallas_call x1, Pallas kernels, on_device(): call(middle_kernel, [((events, width), BF16), ((events, width), BF16), ((...  8.09 us
  transfers between devices with their start and end apart: 6, of which 4 were waited for; matrix products, arithmetic and copies ran while one was open for 5% of the time, Pallas kernels for 6%

profile of v1, /device:TPU:0, one launch (start us, length us, event | category | flops | bytes accessed | tf_op | source)
XLA Modules:
  0.0 249.8 jit_solution(15006478807165021260)
XLA Ops:
  7.2 0.8 copy.25
  8.0 0.7 copy.24
  8.7 0.7 shard_map.147
  9.4 14.3 %all_to_all.22 = s32[32,1,128]{2,1,0:T(1,128)S(1)} all-to-all(s32[32,1,128]{2,1,0:T(1,128)S(1)} %bitcast.77), channel_id=1, replica_groups=mesh['seq'=8,'user'=4] {'seq','user'}, dimensions={0} | all-to-all | bytes 32768 | tf_op jit(solution)/shard_map/all_to_all | solution.py:286
  23.7 0.1 copy.19
  23.8 0.0 copy-start.13
  23.8 0.0 copy-start
  23.8 0.0 copy-start.1
  23.8 10.6 %shard_map.148 = bf16[32,128,128]{2,1,0:T(8,128)(2,1)} custom-call(s32[128,32]{1,0:T(8,128)S(1)} %bitcast.74, bf16[4096,128]{1,0:T(8,128)(2,1)S(1)} %copy-done.2), custom_call_target="tpu_custom_call" | custom-call | flops 1073741824 | bytes 4194304 | tf_op jit(solution)/shard_map/pallas_call | solution.py:302
  34.4 3.4 %all-to-all-start.1 = ((bf16[32,128,128]{2,1,0:T(8,128)(2,1)}), bf16[32,128,128]{2,1,0:T(8,128)(2,1)}, u32[]{:S(2)}, u32[]{:S(2)}) async-start(bf16[32,128,128]{2,1,0:T(8,128)(2,1)} %shard_map.148), calls=%async_computation.1 | async-start | bytes 2097152 | tf_op jit(solution)/shard_map/all_to_all | solution.py:303
  37.8 0.0 all-reduce.3.cloned.1.call-start
  37.9 0.6 fusion.2
  39.8 0.0 copy-start.14
  39.8 0.0 copy-start.4
  39.8 0.1 dynamic-slice_bitcast_fusion.2
  40.0 0.9 maximum_select_fusion
  40.9 0.0 all-reduce.3.cloned.1.call-update
  40.9 0.0 copy-start.7
  40.9 0.0 copy-start.8
  41.0 0.0 copy-start.3
  41.0 3.8 %collective-permute-start = (bf16[128,1024]{1,0:T(8,128)(2,1)S(1)}, bf16[128,1024]{1,0:T(8,128)(2,1)S(1)}, u32[]{:S(2)}, u32[]{:S(2)}) collective-permute-start(bf16[128,1024]{1,0:T(8,128)(2,1)S(1)} %pad_maximum_fusion), channel_id=1, source_target_pairs={{0,4},{4,8},{8,12},{12,16},{16,20},{20,24},{24,28},{1,5},{5,9},{9,... | collective-permute-start | bytes 786440 | tf_op jit(solution)/shard_map/ppermute | solution.py:263
  44.8 0.6 dynamic_slice.23
  45.4 0.7 pad_add_fusion.info_ref
  46.1 9.1 %collective-permute-done.prev_ref = bf16[128,1024]{1,0:T(8,128)(2,1)S(1)} collective-permute-done((bf16[128,1024]{1,0:T(8,128)(2,1)S(1)}, bf16[128,1024]{1,0:T(8,128)(2,1)S(1)}, u32[]{:S(2)}, u32[]{:S(2)}) %collective-permute-start) | collective-permute-done | bytes 262176 | tf_op jit(solution)/shard_map/ppermute | solution.py:263
  55.2 65.9 %all-reduce.3.cloned.1.call-done.glob_ref = bf16[2,128,1024]{2,1,0:T(8,128)(2,1)} async-done(((bf16[2,128,1024]{2,1,0:T(8,128)(2,1)}), bf16[2,128,1024]{2,1,0:T(8,128)(2,1)}) %all-reduce.3.cloned.1.call-update) | async-done | bytes 524304 | tf_op jit(solution)/shard_map/psum | solution.py:299
  121.1 1.0 copy-done.5
  122.1 4.8 %shard_map.146.attn_ref = f32[512,512]{1,0:T(8,128)S(1)} custom-call(s32[4]{0:T(128)S(1)} %pad_add_fusion.info_ref, bf16[512,512]{1,0:T(8,128)(2,1)S(1)} %bitcast.82, bf16[512,512]{1,0:T(8,128)(2,1)S(1)} %bitcast.70, bf16[512,512]{1,0:T(8,128)(2,1)S(1)} %bitcast.72, bf16[128,1024]{1,0:T(8,128)(2,1)S(1)} %collective-permute-done.prev_ref, ...), custom_call_target="tpu_custom_call" | custom-call | flops 1073741824 | bytes 4194304 | tf_op jit(solution)/shard_map/pallas_call | solution.py:305
  126.9 1.0 copy-done.9
  127.9 1.2 copy-done.10
  129.2 8.1 %shard_map.149 = (bf16[512,512]{1,0:T(8,128)(2,1)S(1)}, bf16[512,512]{1,0:T(8,128)(2,1)}, bf16[32,128,128]{2,1,0:T(8,128)(2,1)}) custom-call(s32[4]{0:T(128)S(1)} %pad_add_fusion.info_ref, f32[512,512]{1,0:T(8,128)S(1)} %copy-done.10, bf16[512,512]{1,0:T(8,128)(2,1)S(1)} %bitcast.81, bf16[512,128]{1,0:T(8,128)(2,1)S(1)} %bitcast.84, ...), custom_call_target="tpu_custom_call" | custom-call | flops 1073741824 | bytes 4194304 | tf_op jit(solution)/shard_map/pallas_call | solution.py:308
  137.2 0.8 copy-done.11
  138.0 3.9 %all-to-all-start.2 = ((bf16[32,128,128]{2,1,0:T(8,128)(2,1)}), bf16[32,128,128]{2,1,0:T(8,128)(2,1)S(1)}, u32[]{:S(2)}, u32[]{:S(2)}) async-start(bf16[32,128,128]{2,1,0:T(8,128)(2,1)} %get-tuple-element.34), calls=%async_computation.2 | async-start | bytes 2097152 | tf_op jit(solution)/shard_map/all_to_all | solution.py:313
  141.9 0.3 all-reduce.5.cloned.1.call-start
  142.2 0.0 copy-start.12
  142.2 1.0 copy-done.12
  143.3 10.3 %shard_map.150 = (bf16[512,512]{1,0:T(8,128)(2,1)}, f32[512,1024]{1,0:T(8,128)}, bf16[128,1024]{1,0:T(8,128)(2,1)}, bf16[2,128,1024]{2,1,0:T(8,128)(2,1)}) custom-call(s32[4]{0:T(128)S(1)} %pad_add_fusion.info_ref, bf16[512,512]{1,0:T(8,128)(2,1)S(1)} %bitcast.83, bf16[512,512]{1,0:T(8,128)(2,1)S(1)} %bitcast.71, bf16[512,512]{1,0:T(8,128)(2,1)S(1)} %bitcast.73, ...), custom_call_target="tpu_custom_call" | custom-call | flops 1073741824 | bytes 4194304 | tf_op jit(solution)/shard_map/pallas_call | solution.py:315
  153.6 1.5 collective-permute-start.1
  155.1 0.0 all-reduce.5.cloned.1.call-update
  155.2 0.1 compare_and_fusion
  155.2 3.2 %copy.27 = f32[4,128,1024]{2,1,0:T(8,128)} copy(f32[4,128,1024]{2,1,0:T(8,128)} %bitcast.86) | data formatting | bytes 4194304
  158.4 8.6 %collective-permute-done.1 = bf16[128,1024]{1,0:T(8,128)(2,1)S(1)} collective-permute-done((bf16[128,1024]{1,0:T(8,128)(2,1)}, bf16[128,1024]{1,0:T(8,128)(2,1)S(1)}, u32[]{:S(2)}, u32[]{:S(2)}) %collective-permute-start.1) | collective-permute-done | bytes 262176 | tf_op jit(solution)/shard_map/ppermute | solution.py:263
  167.0 1.9 bitcast_dynamic-update-slice_fusion
  168.9 63.2 %all-reduce.5.cloned.1.call-done = bf16[2,128,1024]{2,1,0:T(8,128)(2,1)} async-done(((bf16[2,128,1024]{2,1,0:T(8,128)(2,1)}), bf16[2,128,1024]{2,1,0:T(8,128)(2,1)}) %all-reduce.5.cloned.1.call-update) | async-done | bytes 524304 | tf_op jit(solution)/shard_map/psum | solution.py:327
  232.1 1.1 convert_element_type.13
  233.3 0.1 slice_bitcast_fusion.3
  233.4 2.0 add_convert_fusion
  235.4 1.0 slice_bitcast_fusion
  236.5 6.5 %shard_map.151 = f32[4096,128]{1,0:T(8,128)} custom-call(s32[128,32]{1,0:T(8,128)S(1)} %bitcast.75, s32[1,4096]{1,0:T(1,128)S(1)} %bitcast.76, bf16[32,128,128]{2,1,0:T(8,128)(2,1)S(1)} %all-to-all-done.2.inc_ref), custom_call_target="tpu_custom_call" | custom-call | flops 1073741824 | bytes 4194304 | tf_op jit(solution)/shard_map/pallas_call | solution.py:334
  (26 shorter events, 0.2 us)
Async XLA Ops:
  7.2 16.6 %copy-start.2 = (bf16[4096,128]{1,0:T(8,128)(2,1)S(1)}, bf16[4096,128]{1,0:T(8,128)(2,1)}, u32[]{:S(2)}) copy-start(bf16[4096,128]{1,0:T(8,128)(2,1)} %table_ref.1) | copy-start | bytes 3145732
  23.8 14.1 %copy-start.13 = (s32[1,2]{1,0:T(1,128)S(1)}, s32[1,2]{1,0:T(1,128)}, u32[]{:S(2)}) copy-start(s32[1,2]{1,0:T(1,128)} %param.22) | copy-start | bytes 28
  23.8 16.0 %copy-start = (bf16[1,512,512]{2,1,0:T(8,128)(2,1)S(1)}, bf16[1,512,512]{2,1,0:T(8,128)(2,1)}, u32[]{:S(2)}) copy-start(bf16[1,512,512]{2,1,0:T(8,128)(2,1)} %param.14) | copy-start | bytes 1572868
  23.8 16.0 %copy-start.1 = (bf16[1,512,512]{2,1,0:T(8,128)(2,1)S(1)}, bf16[1,512,512]{2,1,0:T(8,128)(2,1)}, u32[]{:S(2)}) copy-start(bf16[1,512,512]{2,1,0:T(8,128)(2,1)} %param.15) | copy-start | bytes 1572868
  34.4 93.5 %all-to-all-start.1 = ((bf16[32,128,128]{2,1,0:T(8,128)(2,1)}), bf16[32,128,128]{2,1,0:T(8,128)(2,1)}, u32[]{:S(2)}, u32[]{:S(2)}) async-start(bf16[32,128,128]{2,1,0:T(8,128)(2,1)} %shard_map.148), calls=%async_computation.1 | async-start | bytes 2097152 | tf_op jit(solution)/shard_map/all_to_all | solution.py:303
  37.8 83.2 %all-reduce.3.cloned.1.call-start = ((), (), s32[]{:S(2)}) async-start(), calls=%async_computation.3 | async-start | bytes 1048576 | tf_op jit(solution)/shard_map/psum | solution.py:299
  39.8 5.0 %copy-start.14 = (s32[4]{0:T(128)S(1)}, s32[4]{0:T(128)}, u32[]{:S(2)}) copy-start(s32[4]{0:T(128)} %param.23) | copy-start | bytes 52
  39.8 81.2 %copy-start.4 = (bf16[1,512,512]{2,1,0:T(8,128)(2,1)S(1)}, bf16[1,512,512]{2,1,0:T(8,128)(2,1)}, u32[]{:S(2)}) copy-start(bf16[1,512,512]{2,1,0:T(8,128)(2,1)} %param.13) | copy-start | bytes 1572868
  40.9 87.0 %copy-start.7 = (bf16[1,512,128]{2,1,0:T(8,128)(2,1)S(1)}, bf16[1,512,128]{2,1,0:T(8,128)(2,1)}, u32[]{:S(2)}) copy-start(bf16[1,512,128]{2,1,0:T(8,128)(2,1)} %param.17) | copy-start | bytes 393220
  40.9 87.0 %copy-start.8 = (bf16[512,128]{1,0:T(8,128)(2,1)S(1)}, bf16[512,128]{1,0:T(8,128)(2,1)}, u32[]{:S(2)}) copy-start(bf16[512,128]{1,0:T(8,128)(2,1)} %w_ref.1) | copy-start | bytes 393220
  41.0 87.0 %copy-start.3 = (bf16[1,512,512]{2,1,0:T(8,128)(2,1)S(1)}, bf16[1,512,512]{2,1,0:T(8,128)(2,1)}, u32[]{:S(2)}) copy-start(bf16[1,512,512]{2,1,0:T(8,128)(2,1)} %param.16) | copy-start | bytes 1572868
  41.0 14.2 %collective-permute-start = (bf16[128,1024]{1,0:T(8,128)(2,1)S(1)}, bf16[128,1024]{1,0:T(8,128)(2,1)S(1)}, u32[]{:S(2)}, u32[]{:S(2)}) collective-permute-start(bf16[128,1024]{1,0:T(8,128)(2,1)S(1)} %pad_maximum_fusion), channel_id=1, source_target_pairs={{0,4},{4,8},{8,12},{12,16},{16,20},{20,24},{24,28},{1,5},{5,9},{9,... | collective-permute-start | bytes 786440 | tf_op jit(solution)/shard_map/ppermute | solution.py:263
  121.1 1.0 copy-start.5
  126.9 1.0 copy-start.9
  127.9 1.2 copy-start.10
  129.1 13.1 %copy-start.6 = (bf16[2,128,1024]{2,1,0:T(8,128)(2,1)S(1)}, bf16[2,128,1024]{2,1,0:T(8,128)(2,1)}, u32[]{:S(2)}) copy-start(bf16[2,128,1024]{2,1,0:T(8,128)(2,1)} %all-reduce.3.cloned.1.call-done.glob_ref) | copy-start | bytes 1572868
  137.2 0.8 copy-start.11
  138.0 98.5 %all-to-all-start.2 = ((bf16[32,128,128]{2,1,0:T(8,128)(2,1)}), bf16[32,128,128]{2,1,0:T(8,128)(2,1)S(1)}, u32[]{:S(2)}, u32[]{:S(2)}) async-start(bf16[32,128,128]{2,1,0:T(8,128)(2,1)} %get-tuple-element.34), calls=%async_computation.2 | async-start | bytes 2097152 | tf_op jit(solution)/shard_map/all_to_all | solution.py:313
  141.9 90.2 %all-reduce.5.cloned.1.call-start = ((), (), s32[]{:S(2)}) async-start(), calls=%async_computation.4 | async-start | bytes 1048576 | tf_op jit(solution)/shard_map/psum | solution.py:327
  142.2 1.0 copy-start.12
  153.6 13.4 %collective-permute-start.1 = (bf16[128,1024]{1,0:T(8,128)(2,1)}, bf16[128,1024]{1,0:T(8,128)(2,1)S(1)}, u32[]{:S(2)}, u32[]{:S(2)}) collective-permute-start(bf16[128,1024]{1,0:T(8,128)(2,1)} %get-tuple-element.31), channel_id=1, source_target_pairs={{4,0},{8,4},{12,8},{16,12},{20,16},{24,20},{28,24},{5,1},{9,5},{13... | collective-permute-start | bytes 786440 | tf_op jit(solution)/shard_map/ppermute | solution.py:263
Sparse Core Ops, SparseCore 0:
  42.6 78.3 all-reduce.2
  155.3 76.8 all-reduce.4

commit v2 on v0

v2 whole, which is shorter than its diff:
```python
import functools

import jax
import jax.numpy as jnp
from jax import lax
from jax.experimental import pallas as pl
from jax.experimental.pallas import tpu as pltpu
from jax.sharding import PartitionSpec as P

HEADS = 8
HEAD_DIM = 64
BLK = 128
GLOB = 2
PAIR = 2 * HEAD_DIM
HI = 512
F32 = jnp.float32
BF16 = jnp.bfloat16
VMEM = pl.BlockSpec(memory_space=pltpu.VMEM)
SMEM = pl.BlockSpec(memory_space=pltpu.SMEM)
NT = (((1,), (1,)), ((), ()))
TN = (((0,), (0,)), ((), ()))
LIMIT = 50 * 1024 * 1024


def iota(shape, axis):
    return lax.broadcasted_iota(jnp.int32, shape, axis)


def mm(left, right):
    return jnp.dot(left, right, preferred_element_type=F32)


def dg(left, right, dims):
    return lax.dot_general(left, right, dims, preferred_element_type=F32)


def stack_pair(rows):
    lane = iota(rows.shape, 1)
    zero = jnp.zeros_like(rows)
    return jnp.concatenate(
        [jnp.where(lane < HEAD_DIM, rows, zero), jnp.where(lane < HEAD_DIM, zero, rows)], axis=0
    )


def merge_pair(stacked):
    half = stacked.shape[0] // 2
    lane = iota((half, stacked.shape[1]), 1)
    return jnp.where(lane < HEAD_DIM, stacked[:half], stacked[half:])


def sigmoid(x):
    return 0.5 * jnp.tanh(0.5 * x) + 0.5


def visible(block, length, gids):
    query = iota((2 * BLK, BLK), 0) % BLK
    key = iota((2 * BLK, BLK), 1)
    prev = (key + (block - 1) * BLK < length) & (block > 0)
    own = (key <= query) & (key + block * BLK < length)
    globs = [(key + gid * BLK < length) & (gid < block - 1) for gid in gids]
    return jnp.concatenate([m.astype(F32) for m in [prev, own] + globs], axis=1)


def make_requests(owner_ref, row_ref, ndev, cap):
    events = owner_ref.shape[1]
    dev = iota((ndev, events), 0)
    hits = [owner_ref[j : j + 1, :] == dev for j in range(owner_ref.shape[0])]
    named = functools.reduce(jnp.logical_or, hits)
    upper = (iota((events, events), 0) < iota((events, events), 1)).astype(BF16)
    rank = mm(named.astype(BF16), upper)
    high = jnp.zeros((ndev, cap), F32)
    low = jnp.zeros((ndev, cap), F32)
    place = iota((cap, events), 0)
    for j, hit in enumerate(hits):
        slot = jnp.sum(jnp.where(hit, rank, 0.0), axis=0, keepdims=True).astype(jnp.int32)
        chosen = (place == slot).astype(BF16)
        code = row_ref[j : j + 1, :] + 1
        high += dg(jnp.where(hit, (code // 64).astype(F32), 0.0).astype(BF16), chosen, NT)
        low += dg(jnp.where(hit, (code % 64).astype(F32), 0.0).astype(BF16), chosen, NT)
    requests = (high * 64.0 + low).astype(jnp.int32) - 1
    return jnp.where(named, rank, -1.0).astype(jnp.int32), requests


def column(row):
    n = row.shape[1]
    eye = iota((n, n), 0) == iota((n, n), 1)
    return jnp.sum(jnp.where(eye, row.astype(F32), 0.0), axis=1, keepdims=True).astype(jnp.int32)


def kernel(
    nseq, nuser,
    info_ref, q_ref, k_ref, v_ref, gate_ref, hist_ref, w_ref, table_ref, owner_ref, row_ref,
    dq_ref, dk_ref, dv_ref, d_gate_ref, table_grad_ref,
    ask_out, asked, found, returned, outgoing, incoming, slots_ref, score_ref, weights,
    kv, prev, pieces, rs_in, glob, d_kv, d_glob, d_pieces, rs2_in, glob2, d_prev, edge,
    attn_ref, d_attn_ref, normed_ref,
    req_sems, found_sems, out_sems, prev_sems, edge_sems, rs_sems, ag_sems, rs2_sems, ag2_sems,
):
    ndev = nseq * nuser
    events, width = q_ref.shape
    nbd = events // BLK
    cap, emb = found.shape[1:]
    part_rows = GLOB * BLK // nseq
    s, u = lax.axis_index("seq"), lax.axis_index("user")
    me = s * nuser + u
    base = s * nbd
    length = info_ref[0]
    gids = [info_ref[1 + g] for g in range(GLOB)]

    def remote(src, dst, sems, to):
        return pltpu.make_async_remote_copy(
            src_ref=src, dst_ref=dst, send_sem=sems.at[0], recv_sem=sems.at[1],
            device_id=to, device_id_type=pl.DeviceIdType.MESH,
        )

    def device(d):
        return (d // nuser, lax.rem(d, nuser))

    def peer(i):
        return lax.rem(s + i, nseq)

    def every(n, act):
        lax.fori_loop(0, n, lambda i, _: (act(i), 0)[1], 0)

    def bulk(ref, sems):
        return remote(ref, ref, sems, (lax.rem(s + 1, nseq), u))

    barrier = pltpu.get_barrier_semaphore()

    def greet(i):
        pl.semaphore_signal(
            barrier, inc=1, device_id=device(lax.rem(me + i + 1, ndev)),
            device_id_type=pl.DeviceIdType.MESH,
        )

    every(ndev - 1, greet)
    slots, requests = make_requests(owner_ref, row_ref, ndev, cap)
    slots_ref[...] = slots
    for d in range(ndev):
        ask_out[d] = requests[d : d + 1]
    kv[BLK:, :width] = k_ref[...]
    kv[BLK:, width:] = v_ref[...]
    for g in range(GLOB):
        piece = jnp.zeros((BLK, 2 * width), F32)
        for b in range(nbd):
            held = (gids[g] == base + b).astype(F32)
            piece += kv[(b + 1) * BLK : (b + 2) * BLK, :].astype(F32) * held
        pieces[g * BLK : (g + 1) * BLK, :] = piece.astype(BF16)
    pl.semaphore_wait(barrier, ndev - 1)

    def ask(i):
        d = lax.rem(me + i + 1, ndev)
        remote(ask_out.at[d], asked.at[me], req_sems, device(d)).start()

    every(ndev - 1, ask)
    previous = remote(kv.at[pl.ds(events, BLK)], prev, prev_sems, (lax.rem(s + 1, nseq), u))
    pl.when(s < nseq - 1)(previous.start)

    def scatter_piece(src, dst, sems):
        def send(i):
            to = peer(i + 1)
            rows = pl.ds(pl.multiple_of(to * part_rows, part_rows), part_rows)
            remote(src.at[rows], dst.at[s], sems, (to, u)).start()

        every(nseq - 1, send)

    def share_piece(src, landed, sems_in, whole, sems_out):
        bulk(landed.at[pl.ds(0, nseq - 1)], sems_in).wait_recv()
        mine = pl.ds(pl.multiple_of(s * part_rows, part_rows), part_rows)
        landed[s] = src[mine, :]
        total = landed[0].astype(F32)
        for i in range(1, nseq):
            total += landed[i].astype(F32)
        whole[mine, :] = total.astype(BF16)

        def send(i):
            remote(whole.at[mine], whole.at[mine], sems_out, (peer(i + 1), u)).start()

        every(nseq - 1, send)

    scatter_piece(pieces, rs_in, rs_sems)
    asked[me] = ask_out[me]
    bulk(asked.at[pl.ds(0, ndev - 1)], req_sems).wait_recv()

    table_parts = table_ref.shape[0] // HI

    def rows_for(d):
        want = column(asked[d])
        part = want // HI
        chosen = (jnp.broadcast_to(want - part * HI, (cap, HI)) == iota((cap, HI), 1)).astype(BF16)
        part_b = jnp.broadcast_to(part, (cap, emb))
        rows = jnp.zeros((cap, emb), F32)
        for k in range(table_parts):
            rows = jnp.where(part_b == k, mm(chosen, table_ref[k * HI : (k + 1) * HI, :]), rows)
        return rows.astype(BF16)

    def answer(i):
        d = lax.rem(me + i, ndev)
        found[d] = rows_for(d)
        remote(found.at[d], returned.at[me], found_sems, device(d)).start()

    near = ndev // 4

    def far_first(act):
        every(ndev // 2, lambda i: act(i + near))

    def near_last(act):
        every(near, lambda i: act(i + near + ndev // 2))
        every(near - 1, lambda i: act(i + 1))

    far_first(answer)
    share_piece(pieces, rs_in, rs_sems, glob, ag_sems)
    near_last(answer)
    returned[me] = rows_for(me)

    @pl.when(s > 0)
    def _():
        previous.wait_recv()

    @pl.when(s == 0)
    def _():
        prev[...] = jnp.zeros_like(prev)

    kv[:BLK, :] = prev[...]
    bulk(glob.at[pl.ds(0, (nseq - 1) * part_rows)], ag_sems).wait_recv()

    def at(b, count):
        return pl.ds(pl.multiple_of(b * BLK, BLK), count)

    def keys(b, p):
        cols = slice(p * PAIR, (p + 1) * PAIR)
        return jnp.concatenate([kv[at(b, 2 * BLK), cols], glob[:, cols]], axis=0)

    pairs = width // PAIR

    def forward(b):
        mask = visible(base + b, length, gids)
        for p in range(pairs):
            cols = slice(p * PAIR, (p + 1) * PAIR)
            qs = stack_pair(q_ref[at(b, BLK), cols]) * HEAD_DIM**-0.5
            scores = dg(qs, keys(b, p), NT)
            probs = (scores * sigmoid(scores) * mask).astype(BF16)
            attn_ref[at(b, BLK), cols] = merge_pair(mm(probs, keys(b, pairs + p)))

    every(nbd, forward)

    attn = attn_ref[...]
    centered = attn - jnp.mean(attn, axis=1, keepdims=True)
    inv = lax.rsqrt(jnp.mean(centered * centered, axis=1, keepdims=True) + 1e-05)
    normed = centered * inv
    normed_ref[...] = normed
    gate = gate_ref[...].astype(F32)
    user = mm((normed * gate).astype(BF16), w_ref[...]) + hist_ref[...].astype(F32)
    user_hi = user.astype(BF16)
    user_lo = (user - user_hi.astype(F32)).astype(BF16)
    user_both = jnp.concatenate([user_hi, user_lo], axis=1)
    place = iota((cap, events), 0)

    bulk(returned.at[pl.ds(0, ndev - 1)], found_sems).wait_recv()

    def score_of(i):
        for k in range(4):
            d = i * 4 + k
            rows = returned[d]
            full = dg(jnp.concatenate([rows, rows], axis=1), user_both, NT)
            here = place == slots_ref[pl.ds(d, 1), :]
            score_ref[pl.ds(d, 1), :] = jnp.sum(jnp.where(here, full, 0.0), axis=0, keepdims=True)

    every(ndev // 4, score_of)
    score = score_ref[...]
    positive = owner_ref[0:1, :] == iota((ndev, events), 0)
    first = jnp.sum(jnp.where(positive, score, 0.0), axis=0, keepdims=True)
    valid = base * BLK + iota((ndev, events), 1) < length
    side = jnp.where(
        (slots_ref[...] >= 0) & valid & ~positive, sigmoid(score - first), 0.0
    )
    score_ref[...] = jnp.where(positive, -jnp.sum(side, axis=0, keepdims=True), side)

    def weigh(d):
        here = place == slots_ref[pl.ds(d, 1), :]
        part = jnp.where(here, score_ref[pl.ds(d, 1), :], 0.0).astype(BF16)
        weights[pl.ds(pl.multiple_of(d * cap, cap), cap), :] = part
        return mm(part, user_hi).astype(BF16)

    def give(i):
        d = lax.rem(me + i, ndev)
        outgoing[d] = weigh(d)
        remote(outgoing.at[d], incoming.at[me], out_sems, device(d)).start()

    far_first(give)
    near_last(give)
    incoming[me] = weigh(me)
    d_user = dg(returned[...].reshape(ndev * cap, emb), weights[...], TN)
    d_gated = dg(d_user.T.astype(BF16), w_ref[...], NT)
    normed = normed_ref[...]
    d_gate_ref[...] = (d_gated * normed).astype(BF16)
    dn = d_gated * gate_ref[...].astype(F32)
    shift = jnp.mean(dn, axis=1, keepdims=True)
    d_attn_ref[...] = (
        (dn - shift - normed * jnp.mean(dn * normed, axis=1, keepdims=True)) * inv
    ).astype(BF16)

    d_kv[...] = jnp.zeros_like(d_kv)
    d_glob[...] = jnp.zeros_like(d_glob)

    def backward(b):
        mask = visible(base + b, length, gids)
        for p in range(pairs):
            cols = slice(p * PAIR, (p + 1) * PAIR)
            vcols = slice(width + p * PAIR, width + (p + 1) * PAIR)
            kk = keys(b, p)
            qs = stack_pair(q_ref[at(b, BLK), cols]) * HEAD_DIM**-0.5
            gs = stack_pair(d_attn_ref[at(b, BLK), cols])
            scores = dg(qs, kk, NT)
            sig = sigmoid(scores)
            masked = sig * mask
            probs = (scores * masked).astype(BF16)
            slope = masked * (1.0 + scores * (1.0 - sig))
            d_scores = (dg(gs, keys(b, pairs + p), NT) * slope).astype(BF16)
            dq_ref[at(b, BLK), cols] = (merge_pair(mm(d_scores, kk)) * HEAD_DIM**-0.5).astype(BF16)
            for grad, to in ((dg(d_scores, qs, TN), cols), (dg(probs, gs, TN), vcols)):
                d_kv[at(b, 2 * BLK), to] += grad[: 2 * BLK]
                d_glob[:, to] += grad[2 * BLK :]

    every(nbd, backward)
    d_pieces[...] = d_glob[...].astype(BF16)
    scatter_piece(d_pieces, rs2_in, rs2_sems)
    d_prev[...] = d_kv[:BLK, :].astype(BF16)
    back = remote(d_prev, edge, edge_sems, (lax.rem(s + nseq - 1, nseq), u))
    pl.when(s > 0)(back.start)

    group = 512 // cap
    bulk(incoming.at[pl.ds(0, ndev - 1)], out_sems).wait_recv()
    table_grad_ref[...] = jnp.zeros_like(table_grad_ref)

    def add_rows(i):
        wanted, wide = [], []
        for j in range(group):
            d = i * group + j
            wanted.append(asked[d])
            part_b = jnp.broadcast_to(column(asked[d]), (cap, emb)) // HI
            inc = incoming[d].astype(F32)
            kept = [jnp.where(part_b == k, inc, 0.0).astype(BF16) for k in range(table_parts)]
            wide.append(jnp.concatenate(kept, axis=1))
        row = jnp.concatenate(wanted, axis=1)
        chosen = (row % HI == iota((HI, group * cap), 0)).astype(BF16)
        total = mm(chosen, jnp.concatenate(wide, axis=0))
        for k in range(table_parts):
            table_grad_ref[k * HI : (k + 1) * HI, :] += total[:, k * emb : (k + 1) * emb]

    steps = ndev // group
    every(steps // 2, add_rows)
    share_piece(d_pieces, rs2_in, rs2_sems, glob2, ag2_sems)
    every(steps - steps // 2, lambda i: add_rows(i + steps // 2))

    @pl.when(s < nseq - 1)
    def _():
        back.wait_recv()

    @pl.when(s == nseq - 1)
    def _():
        edge[...] = jnp.zeros_like(edge)

    d_kv[events:, :] += edge[...].astype(F32)
    bulk(glob2.at[pl.ds(0, (nseq - 1) * part_rows)], ag2_sems).wait_recv()
    for b in range(nbd):
        total = d_kv[(b + 1) * BLK : (b + 2) * BLK, :]
        for g in range(GLOB):
            held = (gids[g] == base + b).astype(F32)
            total += glob2[g * BLK : (g + 1) * BLK, :].astype(F32) * held
        dk_ref[b * BLK : (b + 1) * BLK, :] = total[:, :width].astype(BF16)
        dv_ref[b * BLK : (b + 1) * BLK, :] = total[:, width:].astype(BF16)

    pl.when(s < nseq - 1)(previous.wait_send)
    pl.when(s > 0)(back.wait_send)
    for ref, sems, count in (
        (ask_out, req_sems, ndev - 1),
        (found, found_sems, ndev - 1),
        (outgoing, out_sems, ndev - 1),
        (rs_in, rs_sems, nseq - 1),
        (rs2_in, rs2_sems, nseq - 1),
        (glob, ag_sems, (nseq - 1) * part_rows),
        (glob2, ag2_sems, (nseq - 1) * part_rows),
    ):
        bulk(ref.at[pl.ds(0, count)], sems).wait_send()


def on_device(
    query, key, value, gate, history, w_out, table, item_owner, item_row, global_blocks, lengths
):
    events, width = query.shape[1:]
    emb = table.shape[1]
    nseq, nuser = lax.axis_size("seq"), lax.axis_size("user")
    ndev = nseq * nuser
    cap = -(-max(2, 15 * events // (2 * ndev)) // 16) * 16
    length = lax.dynamic_slice_in_dim(lengths, lax.axis_index("user"), 1)
    info = jnp.concatenate([length, global_blocks[0]]).astype(jnp.int32)
    rows = events + BLK
    part_rows = GLOB * BLK // nseq
    outs = [((events, width), BF16)] * 4 + [(table.shape, F32)]
    scratch = [
        ((ndev, 1, cap), jnp.int32), ((ndev, 1, cap), jnp.int32),
        ((ndev, cap, emb), BF16), ((ndev, cap, emb), BF16),
        ((ndev, cap, emb), BF16), ((ndev, cap, emb), BF16),
        ((ndev, events), jnp.int32), ((ndev, events), F32), ((ndev * cap, events), BF16),
        ((rows, 2 * width), BF16), ((BLK, 2 * width), BF16),
        ((GLOB * BLK, 2 * width), BF16), ((nseq, part_rows, 2 * width), BF16),
        ((GLOB * BLK, 2 * width), BF16),
        ((rows, 2 * width), F32), ((GLOB * BLK, 2 * width), F32),
        ((GLOB * BLK, 2 * width), BF16), ((nseq, part_rows, 2 * width), BF16),
        ((GLOB * BLK, 2 * width), BF16),
        ((BLK, 2 * width), BF16), ((BLK, 2 * width), BF16),
        ((events, width), F32), ((events, width), BF16), ((events, width), F32),
    ]
    d_q, d_k, d_v, d_gate, table_grad = pl.pallas_call(
        functools.partial(kernel, nseq, nuser),
        out_shape=[jax.ShapeDtypeStruct(shape, dtype) for shape, dtype in outs],
        in_specs=[SMEM] + [VMEM] * 9,
        out_specs=[VMEM] * len(outs),
        scratch_shapes=[pltpu.VMEM(shape, dtype) for shape, dtype in scratch]
        + [pltpu.SemaphoreType.DMA((2,))] * 9,
        compiler_params=pltpu.CompilerParams(
            vmem_limit_bytes=LIMIT, collective_id=0, has_side_effects=True
        ),
        cost_estimate=pl.CostEstimate(flops=1 << 33, bytes_accessed=1 << 23, transcendentals=0),
    )(
        info, query[0], key[0], value[0], gate[0], history[0], w_out, table,
        item_owner[0].T, item_row[0].T,
    )
    return (d_q[None], d_k[None], d_v[None], d_gate[None], table_grad)


def solution(mesh):
    return jax.shard_map(
        on_device,
        mesh=mesh,
        in_specs=(
            P("user", "seq", None),
            P("user", "seq", None),
            P("user", "seq", None),
            P("user", "seq", None),
            P("user", "seq", None),
            P(),
            P(("seq", "user"), None),
            P("user", "seq", None),
            P("user", "seq", None),
            P("user", None),
            P(),
        ),
        out_specs=(
            P("user", "seq", None),
            P("user", "seq", None),
            P("user", "seq", None),
            P("user", "seq", None),
            P(("seq", "user"), None),
        ),
        check_vma=False,
    )
```

time: 322 us -> 133 us (0.41)
  Pallas kernels: 0 us -> 118 us
  local copies, waits for them, and re-layouts: 100 us -> 11.4 us
  waiting for transfers between devices: 76.3 us -> 0 us
  other arithmetic: 77.1 us -> 1.37 us
  matrix products: 28.8 us -> 0 us
  starting transfers between devices: 22.1 us -> 0 us
  between operations: 16.1 us -> 0.66 us
    pallas_call x0 -> x1, Pallas kernels: none -> 118 us  [on_device(): pl.pallas_call(functools.partial(kernel, nseq, nuser), out_shape=[jax.Sha...]
    psum x2 -> x0, waiting for transfers between devices: 75.7 us -> none  [the longest x1 65.7 us: on_device(): lax.psum(d_glob.astype(jnp.bfloat16), 'seq').astype(jnp.float32)]
    dot_general x10 -> x0, matrix products: 28.8 us -> none  [the longest x6 24.2 us: product(): return jnp.einsum(form, left, right, preferred_element_type=jnp.float32)]
    scatter-add x2 -> x0, other arithmetic: 26.6 us -> none  [the longest x1 25.6 us: on_device(): table_grad = jnp.zeros((table.shape[0], table.shape[1]), jnp.float32).at[...]
    concatenate x7 -> x0, local copies, waits for them, and re-layouts: 25.1 us -> none  [the longest x4 21 us: attend_backward(): jnp.concatenate([d_k.reshape(count, width), d_val.reshape(count, width)],...]
    gather x2 -> x0, local copies, waits for them, and re-layouts: 21.3 us -> none  [the longest x1 13.8 us: on_device(): emb = returned[dest, slot].reshape(events, -1, returned.shape[2])]
    all_to_all x3 -> x0, starting transfers between devices: 14.7 us -> none  [the longest x1 6.01 us: on_device(): lax.all_to_all(found, ('seq', 'user'), split_axis=0, concat_axis=0, tiled...]
    unnamed x68 -> x17, local copies, waits for them, and re-layouts: 20.6 us -> 9.43 us
  transfers between devices with their start and end apart: 7 -> 0, of which waited for: 3 -> 0; matrix products, arithmetic and copies ran while one was open for 35% -> 0% of each run, Pallas kernels for 0% -> 0%
where the time goes in v2:
time: 133 us; the launch traced here: 131 us
  Pallas kernels  118 us (89%)
  local copies, waits for them, and re-layouts  11.4 us (9%)
  other arithmetic  1.37 us (1%)
    pallas_call x1, Pallas kernels, on_device(): pl.pallas_call(functools.partial(kernel, nseq, nuser), out_shape=[jax.Sha...  118 us
    unnamed x17, local copies, waits for them, and re-layouts  9.43 us

profile of v2, /device:TPU:0, one launch (start us, length us, event | category | flops | bytes accessed | tf_op | source)
XLA Modules:
  0.0 131.5 jit_solution(7549003024550556984)
XLA Ops:
  0.6 1.2 dynamic_slice.3
  1.9 1.4 %pad_add_fusion.info_ref = s32[3]{0:T(128)S(1)} fusion(s32[2]{0:T(128)} %bitcast.27, s32[1]{0:T(128)} %dynamic_slice.3), kind=kLoop, calls=%fused_computation.2 | loop fusion | flops 3 | bytes 24 | tf_op jit(solution)/shard_map/concatenate | solution.py:397
  3.3 0.7 copy_bitcast_fusion
  4.0 0.0 copy-start
  4.0 1.0 copy-done
  5.0 0.0 copy-start.1
  5.0 1.0 copy-done.1
  6.1 0.0 copy-start.2
  6.1 1.0 copy-done.2
  7.1 0.0 copy-start.3
  7.1 0.9 copy-done.3
  8.0 0.0 copy-start.4
  8.0 0.9 copy-done.4
  8.9 118.0 %shard_map.146 = (bf16[512,512]{1,0:T(8,128)(2,1)S(1)}, bf16[512,512]{1,0:T(8,128)(2,1)S(1)}, bf16[512,512]{1,0:T(8,128)(2,1)S(1)}, bf16[512,512]{1,0:T(8,128)(2,1)S(1)}, f32[4096,128]{1,0:T(8,128)}) custom-call(s32[3]{0:T(128)S(1)} %pad_add_fusion.info_ref, bf16[512,512]{1,0:T(8,128)(2,1)S(1)} %bitcast.22, bf16[512,512]{1,0:T(8,128)(2,1)S(1)} %bitcast.23, ...), custom_call_target="tpu_custom_call" | custom-call | flops 8589934592 | bytes 8388608 | tf_op jit(solution)/shard_map/pallas_call | solution.py:415
  127.0 0.0 copy-start.5
  127.0 0.8 copy.25
  127.8 0.8 copy.26
  128.6 0.8 copy.27
  129.3 0.8 copy.28
  130.1 0.0 copy-done.5
  130.1 1.3 %copy.29 = f32[4096,128]{1,0:T(8,128)} copy(f32[4096,128]{1,0:T(8,128)S(1)} %copy-done.5) | data formatting | bytes 4194304
Async XLA Ops:
  4.0 1.0 copy-start
  5.0 1.0 copy-start.1
  6.1 1.0 copy-start.2
  7.1 0.9 copy-start.3
  8.0 0.9 copy-start.4
  127.0 3.2 %copy-start.5 = (f32[4096,128]{1,0:T(8,128)S(1)}, f32[4096,128]{1,0:T(8,128)}, u32[]{:S(2)}) copy-start(f32[4096,128]{1,0:T(8,128)} %get-tuple-element.26) | copy-start | bytes 6291460

commit v3 on v2

--- a/solution.py
+++ b/solution.py
@@ -19,7 +19,7 @@
 SMEM = pl.BlockSpec(memory_space=pltpu.SMEM)
 NT = (((1,), (1,)), ((), ()))
 TN = (((0,), (0,)), ((), ()))
-LIMIT = 50 * 1024 * 1024
+LIMIT = 60 * 1024 * 1024
 
 
 def iota(shape, axis):
@@ -89,12 +89,14 @@
 
 def kernel(
     nseq, nuser,
-    info_ref, q_ref, k_ref, v_ref, gate_ref, hist_ref, w_ref, table_ref, owner_ref, row_ref,
+    lengths_ref, gids_ref, q_hbm, k_hbm, v_hbm, gate_hbm, hist_hbm, w_hbm, table_hbm,
+    owner_ref, row_ref,
     dq_ref, dk_ref, dv_ref, d_gate_ref, table_grad_ref,
     ask_out, asked, found, returned, outgoing, incoming, slots_ref, score_ref, weights,
     kv, prev, pieces, rs_in, glob, d_kv, d_glob, d_pieces, rs2_in, glob2, d_prev, edge,
-    attn_ref, d_attn_ref, normed_ref,
+    attn_ref, d_attn_ref, normed_ref, q_ref, gate_ref, hist_ref, w_ref, table_ref,
     req_sems, found_sems, out_sems, prev_sems, edge_sems, rs_sems, ag_sems, rs2_sems, ag2_sems,
+    found_recv, out_recv, load_sems,
 ):
     ndev = nseq * nuser
     events, width = q_ref.shape
@@ -104,14 +106,32 @@
     s, u = lax.axis_index("seq"), lax.axis_index("user")
     me = s * nuser + u
     base = s * nbd
-    length = info_ref[0]
-    gids = [info_ref[1 + g] for g in range(GLOB)]
-
-    def remote(src, dst, sems, to):
+    length = lengths_ref[u]
+    gids = [gids_ref[0, g] for g in range(GLOB)]
+
+    def remote(src, dst, sems, to, landed=None):
         return pltpu.make_async_remote_copy(
-            src_ref=src, dst_ref=dst, send_sem=sems.at[0], recv_sem=sems.at[1],
+            src_ref=src, dst_ref=dst, send_sem=sems.at[0],
+            recv_sem=sems.at[1] if landed is None else landed,
             device_id=to, device_id_type=pl.DeviceIdType.MESH,
         )
+
+    def load(index, src, dst):
+        copy = pltpu.make_async_copy(src, dst, load_sems.at[index])
+        copy.start()
+        return copy
+
+    own = pl.ds(BLK, events)
+    load_k = load(0, k_hbm, kv.at[own, pl.ds(0, width)])
+    load_v = load(1, v_hbm, kv.at[own, pl.ds(width, width)])
+    load_table = load(2, table_hbm, table_ref)
+    load_q = load(3, q_hbm, q_ref)
+    loads = [
+        load(4 + n, src, dst)
+        for n, (src, dst) in enumerate(
+            [(gate_hbm, gate_ref), (hist_hbm, hist_ref), (w_hbm, w_ref)]
+        )
+    ]
 
     def device(d):
         return (d // nuser, lax.rem(d, nuser))
@@ -138,8 +158,8 @@
     slots_ref[...] = slots
     for d in range(ndev):
         ask_out[d] = requests[d : d + 1]
-    kv[BLK:, :width] = k_ref[...]
-    kv[BLK:, width:] = v_ref[...]
+    load_k.wait()
+    load_v.wait()
     for g in range(GLOB):
         piece = jnp.zeros((BLK, 2 * width), F32)
         for b in range(nbd):
@@ -156,31 +176,36 @@
     previous = remote(kv.at[pl.ds(events, BLK)], prev, prev_sems, (lax.rem(s + 1, nseq), u))
     pl.when(s < nseq - 1)(previous.start)
 
-    def scatter_piece(src, dst, sems):
+    half = nseq // 2
+    mine = pl.ds(pl.multiple_of(s * part_rows, part_rows), part_rows)
+
+    def scatter_piece(src, dst, sems, wanted):
         def send(i):
             to = peer(i + 1)
             rows = pl.ds(pl.multiple_of(to * part_rows, part_rows), part_rows)
-            remote(src.at[rows], dst.at[s], sems, (to, u)).start()
+            pl.when(wanted(to))(remote(src.at[rows], dst.at[s], sems, (to, u)).start)
 
         every(nseq - 1, send)
 
-    def share_piece(src, landed, sems_in, whole, sems_out):
-        bulk(landed.at[pl.ds(0, nseq - 1)], sems_in).wait_recv()
-        mine = pl.ds(pl.multiple_of(s * part_rows, part_rows), part_rows)
+    def add_pieces(src, landed, sems, whole):
+        bulk(landed.at[pl.ds(0, nseq - 1)], sems).wait_recv()
         landed[s] = src[mine, :]
         total = landed[0].astype(F32)
         for i in range(1, nseq):
             total += landed[i].astype(F32)
         whole[mine, :] = total.astype(BF16)
 
+    def share_piece(whole, sems, wanted):
         def send(i):
-            remote(whole.at[mine], whole.at[mine], sems_out, (peer(i + 1), u)).start()
+            to = peer(i + 1)
+            pl.when(wanted(to))(remote(whole.at[mine], whole.at[mine], sems, (to, u)).start)
 
         every(nseq - 1, send)
 
-    scatter_piece(pieces, rs_in, rs_sems)
+    scatter_piece(pieces, rs_in, rs_sems, lambda to: (to >= half) | (s == 0))
     asked[me] = ask_out[me]
     bulk(asked.at[pl.ds(0, ndev - 1)], req_sems).wait_recv()
+    load_table.wait()
 
     table_parts = table_ref.shape[0] // HI
 
@@ -197,7 +222,7 @@
     def answer(i):
         d = lax.rem(me + i, ndev)
         found[d] = rows_for(d)
-        remote(found.at[d], returned.at[me], found_sems, device(d)).start()
+        remote(found.at[d], returned.at[me], found_sems, device(d), found_recv.at[i]).start()
 
     near = ndev // 4
 
@@ -209,7 +234,21 @@
         every(near - 1, lambda i: act(i + 1))
 
     far_first(answer)
-    share_piece(pieces, rs_in, rs_sems, glob, ag_sems)
+
+    @pl.when(s >= half)
+    def _():
+        add_pieces(pieces, rs_in, rs_sems, glob)
+
+    @pl.when((s > 0) & (s < half))
+    def _():
+        bulk(rs_in.at[pl.ds(0, 1)], rs_sems).wait_recv()
+        glob[mine, :] = rs_in[0]
+
+    @pl.when(s == 0)
+    def _():
+        glob[mine, :] = pieces[mine, :]
+
+    share_piece(glob, ag_sems, lambda to: to >= 0)
     near_last(answer)
     returned[me] = rows_for(me)
 
@@ -232,6 +271,7 @@
         return jnp.concatenate([kv[at(b, 2 * BLK), cols], glob[:, cols]], axis=0)
 
     pairs = width // PAIR
+    load_q.wait()
 
     def forward(b):
         mask = visible(base + b, length, gids)
@@ -243,6 +283,9 @@
             attn_ref[at(b, BLK), cols] = merge_pair(mm(probs, keys(b, pairs + p)))
 
     every(nbd, forward)
+
+    for copy in loads:
+        copy.wait()
 
     attn = attn_ref[...]
     centered = attn - jnp.mean(attn, axis=1, keepdims=True)
@@ -256,11 +299,18 @@
     user_both = jnp.concatenate([user_hi, user_lo], axis=1)
     place = iota((cap, events), 0)
 
-    bulk(returned.at[pl.ds(0, ndev - 1)], found_sems).wait_recv()
-
-    def score_of(i):
-        for k in range(4):
-            d = i * 4 + k
+    def arrivals(step, count, into, sems, landed):
+        sources = []
+        for k in range(count):
+            i = lax.rem(step * count + k + near, ndev)
+            d = lax.rem(me - i + ndev, ndev)
+            copy = remote(into.at[d], into.at[d], sems, device(d), landed.at[i])
+            pl.when(i != 0)(copy.wait_recv)
+            sources.append(d)
+        return sources
+
+    def score_of(step):
+        for d in arrivals(step, 4, returned, found_sems, found_recv):
             rows = returned[d]
             full = dg(jnp.concatenate([rows, rows], axis=1), user_both, NT)
             here = place == slots_ref[pl.ds(d, 1), :]
@@ -285,7 +335,7 @@
     def give(i):
         d = lax.rem(me + i, ndev)
         outgoing[d] = weigh(d)
-        remote(outgoing.at[d], incoming.at[me], out_sems, device(d)).start()
+        remote(outgoing.at[d], incoming.at[me], out_sems, device(d), out_recv.at[i]).start()
 
     far_first(give)
     near_last(give)
@@ -324,19 +374,17 @@
 
     every(nbd, backward)
     d_pieces[...] = d_glob[...].astype(BF16)
-    scatter_piece(d_pieces, rs2_in, rs2_sems)
+    scatter_piece(d_pieces, rs2_in, rs2_sems, lambda to: to >= 0)
     d_prev[...] = d_kv[:BLK, :].astype(BF16)
     back = remote(d_prev, edge, edge_sems, (lax.rem(s + nseq - 1, nseq), u))
     pl.when(s > 0)(back.start)
 
     group = 512 // cap
-    bulk(incoming.at[pl.ds(0, ndev - 1)], out_sems).wait_recv()
     table_grad_ref[...] = jnp.zeros_like(table_grad_ref)
 
     def add_rows(i):
         wanted, wide = [], []
-        for j in range(group):
-            d = i * group + j
+        for d in arrivals(i, group, incoming, out_sems, out_recv):
             wanted.append(asked[d])
             part_b = jnp.broadcast_to(column(asked[d]), (cap, emb)) // HI
             inc = incoming[d].astype(F32)
@@ -349,9 +397,11 @@
             table_grad_ref[k * HI : (k + 1) * HI, :] += total[:, k * emb : (k + 1) * emb]
 
     steps = ndev // group
-    every(steps // 2, add_rows)
-    share_piece(d_pieces, rs2_in, rs2_sems, glob2, ag2_sems)
-    every(steps - steps // 2, lambda i: add_rows(i + steps // 2))
+    early = steps * 3 // 4
+    every(early, add_rows)
+    add_pieces(d_pieces, rs2_in, rs2_sems, glob2)
+    share_piece(glob2, ag2_sems, lambda to: (to == 0) | (s >= half))
+    every(steps - early, lambda i: add_rows(i + early))
 
     @pl.when(s < nseq - 1)
     def _():
@@ -362,10 +412,26 @@
         edge[...] = jnp.zeros_like(edge)
 
     d_kv[events:, :] += edge[...].astype(F32)
-    bulk(glob2.at[pl.ds(0, (nseq - 1) * part_rows)], ag2_sems).wait_recv()
+    upper = nseq - half
+
+    def of_pieces(cond, ref, sems, count, received):
+        if count:
+            copy = bulk(ref.at[pl.ds(0, count * part_rows)], sems)
+            pl.when(cond)(copy.wait_recv if received else copy.wait_send)
+
+    of_pieces(s == 0, glob2, ag2_sems, nseq - 1, True)
+    of_pieces((s > 0) & (s < half), glob2, ag2_sems, upper, True)
+    of_pieces(s >= half, glob2, ag2_sems, upper - 1, True)
+
+    @pl.when(s == 0)
+    def _():
+        for b in range(nbd):
+            held = (gids[0] == b).astype(F32)
+            d_kv[(b + 1) * BLK : (b + 2) * BLK, :] += glob2[:BLK, :].astype(F32) * held
+
     for b in range(nbd):
         total = d_kv[(b + 1) * BLK : (b + 2) * BLK, :]
-        for g in range(GLOB):
+        for g in range(1, GLOB):
             held = (gids[g] == base + b).astype(F32)
             total += glob2[g * BLK : (g + 1) * BLK, :].astype(F32) * held
         dk_ref[b * BLK : (b + 1) * BLK, :] = total[:, :width].astype(BF16)
@@ -377,12 +443,15 @@
         (ask_out, req_sems, ndev - 1),
         (found, found_sems, ndev - 1),
         (outgoing, out_sems, ndev - 1),
-        (rs_in, rs_sems, nseq - 1),
         (rs2_in, rs2_sems, nseq - 1),
         (glob, ag_sems, (nseq - 1) * part_rows),
-        (glob2, ag2_sems, (nseq - 1) * part_rows),
     ):
         bulk(ref.at[pl.ds(0, count)], sems).wait_send()
+    of_pieces(s == 0, pieces, rs_sems, nseq - 1, False)
+    of_pieces((s > 0) & (s < half), pieces, rs_sems, upper, False)
+    of_pieces(s >= half, pieces, rs_sems, upper - 1, False)
+    of_pieces((s > 0) & (s < half), glob2, ag2_sems, 1, False)
+    of_pieces(s >= half, glob2, ag2_sems, nseq - 1, False)
 
 
 def on_device(
@@ -393,8 +462,6 @@
     nseq, nuser = lax.axis_size("seq"), lax.axis_size("user")
     ndev = nseq * nuser
     cap = -(-max(2, 15 * events // (2 * ndev)) // 16) * 16
-    length = lax.dynamic_slice_in_dim(lengths, lax.axis_index("user"), 1)
-    info = jnp.concatenate([length, global_blocks[0]]).astype(jnp.int32)
     rows = events + BLK
     part_rows = GLOB * BLK // nseq
     outs = [((events, width), BF16)] * 4 + [(table.shape, F32)]
@@ -411,20 +478,23 @@
         ((GLOB * BLK, 2 * width), BF16),
         ((BLK, 2 * width), BF16), ((BLK, 2 * width), BF16),
         ((events, width), F32), ((events, width), BF16), ((events, width), F32),
+        ((events, width), BF16), ((events, width), BF16), ((events, emb), BF16),
+        (w_out.shape, BF16), (table.shape, BF16),
     ]
     d_q, d_k, d_v, d_gate, table_grad = pl.pallas_call(
         functools.partial(kernel, nseq, nuser),
         out_shape=[jax.ShapeDtypeStruct(shape, dtype) for shape, dtype in outs],
-        in_specs=[SMEM] + [VMEM] * 9,
+        in_specs=[SMEM] * 2 + [pl.BlockSpec(memory_space=pl.ANY)] * 7 + [VMEM] * 2,
         out_specs=[VMEM] * len(outs),
         scratch_shapes=[pltpu.VMEM(shape, dtype) for shape, dtype in scratch]
-        + [pltpu.SemaphoreType.DMA((2,))] * 9,
+        + [pltpu.SemaphoreType.DMA((2,))] * 9
+        + [pltpu.SemaphoreType.DMA((n,)) for n in (ndev, ndev, 7)],
         compiler_params=pltpu.CompilerParams(
             vmem_limit_bytes=LIMIT, collective_id=0, has_side_effects=True
         ),
         cost_estimate=pl.CostEstimate(flops=1 << 33, bytes_accessed=1 << 23, transcendentals=0),
     )(
-        info, query[0], key[0], value[0], gate[0], history[0], w_out, table,
+        lengths, global_blocks, query[0], key[0], value[0], gate[0], history[0], w_out, table,
         item_owner[0].T, item_row[0].T,
     )
     return (d_q[None], d_k[None], d_v[None], d_gate[None], table_grad)

time: 133 us -> 128 us (0.962)
  local copies, waits for them, and re-layouts: 11.4 us -> 8.14 us
  other arithmetic: 1.37 us -> 0 us
    unnamed x17 -> x11, local copies, waits for them, and re-layouts: 9.43 us -> 6.8 us
    concatenate x1 -> x0, other arithmetic: 1.37 us -> none  [on_device(): info = jnp.concatenate([length, global_blocks[0]]).astype(jnp.int32)]
where the time goes in v3:
time: 128 us; the launch traced here: 127 us
  Pallas kernels  119 us (93%)
  local copies, waits for them, and re-layouts  8.14 us (6%)
    pallas_call x1, Pallas kernels, on_device(): pl.pallas_call(functools.partial(kernel, nseq, nuser), out_shape=[jax.Sha...  119 us
    unnamed x11, local copies, waits for them, and re-layouts  6.8 us

profile of v3, /device:TPU:0, one launch (start us, length us, event | category | flops | bytes accessed | tf_op | source)
XLA Modules:
  0.0 127.4 jit_solution(12568086226265876039)
XLA Ops:
  0.6 1.3 %copy_bitcast_fusion = (s32[5,512]{1,0:T(8,128)}, s32[5,512]{1,0:T(8,128)}) fusion(s32[1,512,5]{1,0,2:T(1,128)} %param.19, s32[1,512,5]{1,0,2:T(1,128)} %param.18), kind=kLoop, calls=%fused_computation | loop fusion | bytes 40960 | tf_op jit(solution)/shard_map/transpose | solution.py:498
  2.0 118.6 %shard_map.146 = (bf16[512,512]{1,0:T(8,128)(2,1)}, bf16[512,512]{1,0:T(8,128)(2,1)}, bf16[512,512]{1,0:T(8,128)(2,1)}, bf16[512,512]{1,0:T(8,128)(2,1)}, f32[4096,128]{1,0:T(8,128)}) custom-call(s32[4]{0:T(128)} %lengths_ref.1, s32[1,2]{1,0:T(1,128)} %gids_ref.1, bf16[512,512]{1,0:T(8,128)(2,1)} %bitcast.21, bf16[512,512]{1,0:T(8,128)(2,1)} %bitcast.22, ...), custom_call_target="tpu_custom_call" | custom-call | flops 8589934592 | bytes 8388608 | tf_op jit(solution)/shard_map/pallas_call | solution.py:484
  120.6 0.0 copy-start.2
  120.6 0.0 copy-start.1
  120.6 0.0 copy-start
  120.6 2.0 %copy.25 = bf16[1,512,512]{2,1,0:T(8,128)(2,1)} copy(bf16[1,512,512]{2,1,0:T(8,128)(2,1)} %bitcast.20) | data formatting | bytes 1048576
  122.6 1.9 %copy.26 = bf16[1,512,512]{2,1,0:T(8,128)(2,1)} copy(bf16[1,512,512]{2,1,0:T(8,128)(2,1)} %bitcast.19) | data formatting | bytes 1048576
  124.5 0.0 copy-done.2
  124.5 0.8 copy.27
  125.3 0.0 copy-done.1
  125.3 0.8 copy.28
  126.1 0.0 copy-done
  126.1 1.3 %copy.29 = f32[4096,128]{1,0:T(8,128)} copy(f32[4096,128]{1,0:T(8,128)S(1)} %copy-done) | data formatting | bytes 4194304
Async XLA Ops:
  120.6 3.9 %copy-start.2 = (bf16[512,512]{1,0:T(8,128)(2,1)S(1)}, bf16[512,512]{1,0:T(8,128)(2,1)}, u32[]{:S(2)}) copy-start(bf16[512,512]{1,0:T(8,128)(2,1)} %get-tuple-element.12) | copy-start | bytes 1572868
  120.6 4.7 %copy-start.1 = (bf16[512,512]{1,0:T(8,128)(2,1)S(1)}, bf16[512,512]{1,0:T(8,128)(2,1)}, u32[]{:S(2)}) copy-start(bf16[512,512]{1,0:T(8,128)(2,1)} %get-tuple-element.13) | copy-start | bytes 1572868
  120.6 5.5 %copy-start = (f32[4096,128]{1,0:T(8,128)S(1)}, f32[4096,128]{1,0:T(8,128)}, u32[]{:S(2)}) copy-start(f32[4096,128]{1,0:T(8,128)} %get-tuple-element.26) | copy-start | bytes 6291460
